TPU v7x, 32 devices: a whole 2x2x4 slice. The times are simulated.
32 devices in a mesh: group: 8 (over z, core), inner: 4 (over y, x).
Axes of the slice: x: 2, y: 2, z: 4, core: 2. Of those that a mesh axis runs over, the one named last changes fastest.
Arguments:
- leaf_blocks: float32 [8192, 256], P(('group', 'inner')), may hold values from -3 to 3, as said below
- bases: float32 [8192, 320], P(('group', 'inner')), may hold values from -2 to 2
- targets: float32 [8192, 128], P(('group', 'inner')), may hold values from -30 to 30
- coupling: float32 [5, 64], replicated, may hold values from 0.01 to 1
Outputs:
- solution: float32 [8192, 128], P(('group', 'inner'))
Inputs may be any that keep to these rules, and one draw needn't show every extreme that they name: Each leaf block of leaf_blocks is symmetric with all eigenvalues at least 0.4.
All inputs are finite; a program needn't handle non-finite values.
Results may differ from a plain program's by a relative error of at most 0.00014.
Values sent between devices are 32-bit elements; how exact they have to be, the bound alone decides.
A program may use at most 64 MiB of HBM per device.

v0:
```python
import jax
import jax.numpy as jnp
from jax import lax
from jax.sharding import PartitionSpec as P


def from_partner(value, axis, distance):
    mask = 2**distance
    pairs = [(source, source ^ mask) for source in range(lax.axis_size(axis))]
    return lax.ppermute(value, axis, pairs)


def chol_solve(factor, rhs_cols):
    forward = lax.linalg.triangular_solve(factor, rhs_cols, left_side=True, lower=True)
    return lax.linalg.triangular_solve(
        factor, forward, left_side=True, lower=True, transpose_a=True
    )


def coefficients(gram_part, weights, projected):
    capacity = gram_part + jnp.diag(1.0 / weights)
    capacity = 0.5 * (capacity + capacity.T)
    return chol_solve(jnp.linalg.cholesky(capacity), projected)


def contract(first_arg, second_arg):
    return lax.dot_general(
        first_arg, second_arg, (((0,), (0,)), ((), ())), precision=lax.Precision.HIGHEST
    )


def matmul(first_arg, second_arg):
    return jnp.dot(first_arg, second_arg, precision=lax.Precision.HIGHEST)


def pair_step(partial_value, which_bit, inner_bits):
    if which_bit < inner_bits:
        return partial_value + from_partner(partial_value, "inner", which_bit)
    return partial_value + from_partner(partial_value, "group", which_bit - inner_bits)


def per_device(leaf_blocks, bases, targets, coupling):
    low_rank = coupling.shape[1]
    levels = coupling.shape[0]
    inner_bits = lax.axis_size("inner").bit_length() - 1
    factor = jnp.linalg.cholesky(leaf_blocks)
    solved = chol_solve(factor, jnp.concatenate([bases, targets], axis=1))
    partial_value = contract(bases, solved)
    for current in range(levels):
        partial_value = pair_step(partial_value, current, inner_bits)
        solve_coef = coefficients(
            partial_value[:low_rank, :low_rank],
            coupling[current],
            partial_value[:low_rank, low_rank:],
        )
        solved = solved[:, low_rank:] - matmul(solved[:, :low_rank], solve_coef)
        partial_value = partial_value[low_rank:, low_rank:] - matmul(
            partial_value[low_rank:, :low_rank], solve_coef
        )
    return solved


def solution(mesh):
    in_specs = (
        P(("group", "inner"), None),
        P(("group", "inner"), None),
        P(("group", "inner"), None),
        P(),
    )
    out_specs = P(("group", "inner"), None)
    return jax.shard_map(
        per_device, mesh=mesh, in_specs=in_specs, out_specs=out_specs, check_vma=False
    )
```

profile of v0, /device:TPU:0, one launch (start us, length us, event | category | flops | bytes accessed | tf_op | source)
XLA Modules:
  0.0 175.5 jit_solution(15225563569795047958)
XLA Ops:
  0.0 1.1 copy.36
  1.2 11.7 %cholesky.64 = f32[128,128]{1,0:T(8,128)S(1)} custom-call(f32[128,128]{1,0:T(8,128)S(1)} %cholesky.260), custom_call_target="Cholesky" | custom-call | tf_op jit(solution)/shard_map/jit(cholesky)/cholesky | solution.py:46
  13.0 9.8 %custom-call.43 = f32[1,128,128]{1,2,0:T(8,128)S(1)} custom-call(f32[1,128,128]{2,1,0:T(8,128)S(1)} %get-tuple-element.27), custom_call_target="InvertDiagBlocksLowerTriangular" | custom-call | tf_op jit(solution)/shard_map/jit(cholesky)/cholesky | solution.py:46
  23.0 0.3 convolution_subtract_fusion.7
  23.3 11.7 %cholesky.132 = f32[128,128]{1,0:T(8,128)S(1)} custom-call(f32[128,128]{1,0:T(8,128)S(1)} %convolution_subtract_fusion.7), custom_call_target="Cholesky" | custom-call | tf_op jit(solution)/shard_map/jit(cholesky)/cholesky | solution.py:46
  35.1 0.7 compare_reduce_fusion.5
  37.2 4.1 %while.1 = (s32[]{:T(128)}, f32[256,256]{1,0:T(8,128)S(1)}, s32[2,2]{1,0:T(2,128)S(1)}, f32[2,128,128]{2,1,0:T(8,128)S(1)}, s32[]{:T(128)}) while((s32[]{:T(128)}, f32[256,256]{1,0:T(8,128)S(1)}, s32[2,2]{1,0:T(2,128)S(1)}, f32[2,128,128]{2,1,0:T(8,128)S(1)}, s32[]{:T(128)}) %tuple.28), condition=%wide.while_cond, body=%wide.while_body.sunk | while | flops 2 | bytes 131181 | solution.py:15
  37.2 0.7 fusion.102
  37.8 1.3 bitcast_dynamic-update-slice_fusion.2
  39.2 0.7 fusion.102
  39.9 1.3 bitcast_dynamic-update-slice_fusion.2
  41.2 19.9 %custom-call.44 = f32[2,128,128]{1,2,0:T(8,128)S(1)} custom-call(f32[2,128,128]{2,1,0:T(8,128)S(1)} %get-tuple-element.13), custom_call_target="InvertDiagBlocksLowerTriangular" | custom-call | tf_op jit(solution)/shard_map/triangular_solve | solution.py:15
  61.2 0.3 fusion.3
  61.5 0.4 convolution_subtract_fusion.4
  61.9 0.5 fusion.34
  62.4 0.6 fusion.33
  63.0 0.3 convolution_subtract_fusion.3
  63.3 0.4 fusion.32
  63.7 0.9 convolution_bitcast_fusion
  64.6 0.2 copy.39
  64.8 3.0 %collective-permute-start = (f32[320,448]{1,0:T(8,128)S(1)}, f32[320,448]{1,0:T(8,128)S(1)}, u32[]{:S(2)}, u32[]{:S(2)}) collective-permute-start(f32[320,448]{1,0:T(8,128)S(1)} %copy.39), channel_id=1, source_target_pairs={{0,1},{1,0},{2,3},{3,2},{4,5},{5,4},{6,7},{7,6},{8,9},{9,8},{10,11... | collective-permute-start | bytes 1720328 | tf_op jit(solution)/shard_map/ppermute | solution.py:10
  67.8 14.7 %collective-permute-done = f32[320,448]{1,0:T(8,128)S(1)} collective-permute-done((f32[320,448]{1,0:T(8,128)S(1)}, f32[320,448]{1,0:T(8,128)S(1)}, u32[]{:S(2)}, u32[]{:S(2)}) %collective-permute-start) | collective-permute-done | bytes 573472 | tf_op jit(solution)/shard_map/ppermute | solution.py:10
  83.1 5.8 %cholesky.207 = f32[64,64]{1,0:T(8,128)S(1)} custom-call(f32[64,64]{1,0:T(8,128)S(1)} %fusion.73), custom_call_target="Cholesky" | custom-call | tf_op jit(solution)/shard_map/jit(cholesky)/cholesky | solution.py:23
  89.0 0.6 compare_reduce_fusion.4
  89.6 0.7 fusion.37
  90.3 4.9 %custom-call.45 = f32[1,64,64]{1,2,0:T(8,128)S(1)} custom-call(f32[1,64,64]{2,1,0:T(8,128)S(1)} %fusion.37), custom_call_target="InvertDiagBlocksLowerTriangular" | custom-call | tf_op jit(solution)/shard_map/triangular_solve | solution.py:15
  95.2 0.4 fusion.5
  95.9 0.6 slice_subtract_fusion
  96.4 1.8 %collective-permute-start.1 = (f32[256,384]{0,1:T(8,128)S(1)}, f32[256,384]{0,1:T(8,128)S(1)}, u32[]{:S(2)}, u32[]{:S(2)}) collective-permute-start(f32[256,384]{0,1:T(8,128)S(1)} %slice_subtract_fusion), channel_id=1, source_target_pairs={{0,2},{1,3},{2,0},{3,1},{4,6},{5,7},{6,4},{7,5},{8,10},{9,11},{10,... | collective-permute-start | bytes 1179656 | tf_op jit(solution)/shard_map/ppermute | solution.py:10
  98.4 8.4 %collective-permute-done.1 = f32[256,384]{0,1:T(8,128)S(1)} collective-permute-done((f32[256,384]{0,1:T(8,128)S(1)}, f32[256,384]{0,1:T(8,128)S(1)}, u32[]{:S(2)}, u32[]{:S(2)}) %collective-permute-start.1) | collective-permute-done | bytes 393248 | tf_op jit(solution)/shard_map/ppermute | solution.py:10
  107.1 5.8 %cholesky.218 = f32[64,64]{1,0:T(8,128)S(1)} custom-call(f32[64,64]{1,0:T(8,128)S(1)} %fusion.68), custom_call_target="Cholesky" | custom-call | tf_op jit(solution)/shard_map/jit(cholesky)/cholesky | solution.py:23
  112.9 0.6 compare_reduce_fusion.3
  113.6 0.7 fusion.38
  114.3 4.9 %custom-call.46 = f32[1,64,64]{1,2,0:T(8,128)S(1)} custom-call(f32[1,64,64]{2,1,0:T(8,128)S(1)} %fusion.38), custom_call_target="InvertDiagBlocksLowerTriangular" | custom-call | tf_op jit(solution)/shard_map/triangular_solve | solution.py:15
  119.1 0.4 fusion.7
  119.7 0.5 slice_subtract_fusion.1
  120.3 0.5 convolution_subtract_fusion
  120.9 0.5 convolution_subtract_fusion.1
  121.3 0.6 collective-permute-done.2
  122.2 5.8 %cholesky.229 = f32[64,64]{1,0:T(8,128)S(1)} custom-call(f32[64,64]{1,0:T(8,128)S(1)} %fusion.63), custom_call_target="Cholesky" | custom-call | tf_op jit(solution)/shard_map/jit(cholesky)/cholesky | solution.py:23
  128.1 0.6 compare_reduce_fusion.2
  128.7 0.7 fusion.39
  129.4 5.0 %custom-call.47 = f32[1,64,64]{1,2,0:T(8,128)S(1)} custom-call(f32[1,64,64]{2,1,0:T(8,128)S(1)} %fusion.39), custom_call_target="InvertDiagBlocksLowerTriangular" | custom-call | tf_op jit(solution)/shard_map/triangular_solve | solution.py:15
  134.4 0.3 fusion.9
  135.0 0.4 slice_subtract_fusion.2
  135.4 1.5 collective-permute-start.3
  136.9 0.4 convolution_subtract_fusion.2
  137.4 3.6 %collective-permute-done.3 = f32[128,256]{0,1:T(8,128)S(1)} collective-permute-done((f32[128,256]{0,1:T(8,128)S(1)}, f32[128,256]{0,1:T(8,128)S(1)}, u32[]{:S(2)}, u32[]{:S(2)}) %collective-permute-start.3) | collective-permute-done | bytes 131104 | tf_op jit(solution)/shard_map/ppermute | solution.py:10
  141.3 5.9 %cholesky.240 = f32[64,64]{1,0:T(8,128)S(1)} custom-call(f32[64,64]{1,0:T(8,128)S(1)} %copy.60), custom_call_target="Cholesky" | custom-call | tf_op jit(solution)/shard_map/jit(cholesky)/cholesky | solution.py:23
  147.2 0.6 compare_reduce_fusion.1
  147.8 0.7 fusion.40
  148.5 4.9 %custom-call.48 = f32[1,64,64]{1,2,0:T(8,128)S(1)} custom-call(f32[1,64,64]{2,1,0:T(8,128)S(1)} %fusion.40), custom_call_target="InvertDiagBlocksLowerTriangular" | custom-call | tf_op jit(solution)/shard_map/triangular_solve | solution.py:15
  153.4 0.4 fusion.11
  154.0 0.4 slice_subtract_fusion.3
  154.3 2.6 %collective-permute-start.4 = (f32[64,192]{0,1:T(8,128)S(1)}, f32[64,192]{0,1:T(8,128)S(1)}, u32[]{:S(2)}, u32[]{:S(2)}) collective-permute-start(f32[64,192]{0,1:T(8,128)S(1)} %slice_subtract_fusion.3), channel_id=1, source_target_pairs={{0,16},{4,20},{8,24},{12,28},{16,0},{20,4},{24,8},{28,12},{1,17},{... | collective-permute-start | bytes 147464 | tf_op jit(solution)/shard_map/ppermute | solution.py:10
  156.9 0.4 convolution_subtract_fusion.5
  157.3 4.2 %collective-permute-done.4 = f32[64,192]{0,1:T(8,128)S(1)} collective-permute-done((f32[64,192]{0,1:T(8,128)S(1)}, f32[64,192]{0,1:T(8,128)S(1)}, u32[]{:S(2)}, u32[]{:S(2)}) %collective-permute-start.4) | collective-permute-done | bytes 49184 | tf_op jit(solution)/shard_map/ppermute | solution.py:10
  161.9 5.9 %cholesky.251 = f32[64,64]{1,0:T(8,128)S(1)} custom-call(f32[64,64]{1,0:T(8,128)S(1)} %copy.66), custom_call_target="Cholesky" | custom-call | tf_op jit(solution)/shard_map/jit(cholesky)/cholesky | solution.py:23
  167.8 0.6 compare_reduce_fusion
  168.4 0.7 fusion.41
  169.1 4.9 %custom-call.49 = f32[1,64,64]{1,2,0:T(8,128)S(1)} custom-call(f32[1,64,64]{2,1,0:T(8,128)S(1)} %fusion.41), custom_call_target="InvertDiagBlocksLowerTriangular" | custom-call | tf_op jit(solution)/shard_map/triangular_solve | solution.py:15
  174.0 0.3 fusion.15
  174.4 0.3 convolution_subtract_fusion.6
  174.7 0.8 copy.68
  (70 shorter events, 3.6 us)
Async XLA Ops:
  0.0 1.2 copy-start.1
  37.0 24.1 %copy-start.2 = (f32[256,128]{1,0:T(8,128)S(1)}, f32[256,128]{1,0:T(8,128)}, u32[]{:S(2)}) copy-start(f32[256,128]{1,0:T(8,128)} %param.7) | copy-start | bytes 393220
  37.2 24.0 %copy-start = (f32[256,320]{0,1:T(8,128)S(1)}, f32[256,320]{0,1:T(8,128)}, u32[]{:S(2)}) copy-start(f32[256,320]{0,1:T(8,128)} %param.6) | copy-start | bytes 983044
  64.6 3.3 %copy-start.3 = (f32[5,64]{1,0:T(8,128)S(1)}, f32[5,64]{1,0:T(8,128)}, u32[]{:S(2)}) copy-start(f32[5,64]{1,0:T(8,128)} %param.8) | copy-start | bytes 3844
  64.8 17.7 %collective-permute-start = (f32[320,448]{1,0:T(8,128)S(1)}, f32[320,448]{1,0:T(8,128)S(1)}, u32[]{:S(2)}, u32[]{:S(2)}) collective-permute-start(f32[320,448]{1,0:T(8,128)S(1)} %copy.39), channel_id=1, source_target_pairs={{0,1},{1,0},{2,3},{3,2},{4,5},{5,4},{6,7},{7,6},{8,9},{9,8},{10,11... | collective-permute-start | bytes 1720328 | tf_op jit(solution)/shard_map/ppermute | solution.py:10
  96.4 10.4 %collective-permute-start.1 = (f32[256,384]{0,1:T(8,128)S(1)}, f32[256,384]{0,1:T(8,128)S(1)}, u32[]{:S(2)}, u32[]{:S(2)}) collective-permute-start(f32[256,384]{0,1:T(8,128)S(1)} %slice_subtract_fusion), channel_id=1, source_target_pairs={{0,2},{1,3},{2,0},{3,1},{4,6},{5,7},{6,4},{7,5},{8,10},{9,11},{10,... | collective-permute-start | bytes 1179656 | tf_op jit(solution)/shard_map/ppermute | solution.py:10
  120.3 1.7 collective-permute-start.2
  135.4 5.6 %collective-permute-start.3 = (f32[128,256]{0,1:T(8,128)S(1)}, f32[128,256]{0,1:T(8,128)S(1)}, u32[]{:S(2)}, u32[]{:S(2)}) collective-permute-start(f32[128,256]{0,1:T(8,128)S(1)} %slice_subtract_fusion.2), channel_id=1, source_target_pairs={{0,8},{4,12},{8,0},{12,4},{16,24},{20,28},{24,16},{28,20},{1,9},{5... | collective-permute-start | bytes 393224 | tf_op jit(solution)/shard_map/ppermute | solution.py:10
  154.3 7.1 %collective-permute-start.4 = (f32[64,192]{0,1:T(8,128)S(1)}, f32[64,192]{0,1:T(8,128)S(1)}, u32[]{:S(2)}, u32[]{:S(2)}) collective-permute-start(f32[64,192]{0,1:T(8,128)S(1)} %slice_subtract_fusion.3), channel_id=1, source_target_pairs={{0,16},{4,20},{8,24},{12,28},{16,0},{20,4},{24,8},{28,12},{1,17},{... | collective-permute-start | bytes 147464 | tf_op jit(solution)/shard_map/ppermute | solution.py:10
where the time goes:
time: 176 us
  other arithmetic  115 us (65%)
  waiting for transfers between devices  31.6 us (18%)
  matrix products  10.4 us (6%)
  starting transfers between devices  9 us (5%)
  local copies, waits for them, and re-layouts  7.7 us (4%)
  between operations  1.82 us (1%)
    another operation x13, other arithmetic, chol_solve(): lax.linalg.triangular_solve(factor, forward, left_side=True, lower=True,...  47.8 us
    another operation x6, other arithmetic, per_device(): factor = jnp.linalg.cholesky(leaf_blocks)  34 us
    another operation x15, other arithmetic, coefficients(): return chol_solve(jnp.linalg.cholesky(capacity), projected)  32.6 us
    ppermute x5, waiting for transfers between devices, from_partner(): return lax.ppermute(value, axis, pairs)  31.6 us
    ppermute x5, starting transfers between devices, from_partner(): return lax.ppermute(value, axis, pairs)  9 us
    another operation x6, local copies, waits for them, and re-layouts  4.02 us
    dot_general x9, matrix products, matmul(): return jnp.dot(first_arg, second_arg, precision=lax.Precision.HIGHEST)  3.95 us
  transfers between devices with their start and end apart: 5, of which 5 were waited for; matrix products, arithmetic and copies ran while one was open for 1% of the time, Pallas kernels for 0%

commit v1 on v0

v1 whole, which is shorter than its diff:
```python
import functools

import jax
import jax.numpy as jnp
from jax import lax
from jax.experimental import pallas as pl
from jax.experimental.pallas import tpu as pltpu
from jax.sharding import PartitionSpec as P

EIGEN_MIN = 0.4
LEAF_TOL = 3e-4
VMEM = pl.BlockSpec(memory_space=pltpu.VMEM)


def mm(first, second):
    return jnp.dot(
        first,
        second,
        precision=lax.Precision.HIGHEST,
        preferred_element_type=jnp.float32,
    )


def mm_t(first, second):
    return lax.dot_general(
        first,
        second,
        (((0,), (0,)), ((), ())),
        precision=lax.Precision.HIGHEST,
        preferred_element_type=jnp.float32,
    )


def identity(size):
    rows = lax.broadcasted_iota(jnp.int32, (size, size), 0)
    cols = lax.broadcasted_iota(jnp.int32, (size, size), 1)
    return jnp.where(rows == cols, 1.0, 0.0).astype(jnp.float32)


def spd_inverse(matrix, low, high, pair_ref):
    size = matrix.shape[0]
    eye = identity(size)
    alpha = 2.0 / (low + high)
    pair_ref[:size, :] = eye - alpha * matrix
    pair_ref[size:, :] = alpha * eye

    def cond(rho):
        return rho > LEAF_TOL

    def body(rho):
        square = rho * rho
        scale = 2.0 / (2.0 - square)
        pair = pair_ref[...]
        product = mm(pair, pair[:size])
        pair_ref[:size, :] = (1.0 - scale) * eye + scale * product[:size]
        pair_ref[size:, :] = scale * (pair[size:] + product[size:])
        return square / (2.0 - square)

    lax.while_loop(cond, body, (high - low) / (high + low))
    inverse = pair_ref[size:, :]
    return inverse + mm(inverse, eye - mm(matrix, inverse))


def leaf_kernel(rank, levels, leaf_ref, bases_ref, targets_ref, solved_ref, *rest):
    blocks, pair_ref = rest[:levels], rest[levels]
    matrix = leaf_ref[...]
    high = jnp.max(jnp.sum(jnp.abs(matrix), axis=0, keepdims=True))
    inverse = spd_inverse(matrix, EIGEN_MIN, jnp.maximum(high, 2 * EIGEN_MIN), pair_ref)
    columns = [targets_ref[...]] + [
        bases_ref[:, rank * level : rank * (level + 1)]
        for level in reversed(range(levels))
    ]
    rhs = jnp.concatenate(columns, axis=1)
    solved = mm(inverse, rhs)
    solved_ref[...] = solved
    gram = mm_t(bases_ref[...], solved)
    for level in range(levels):
        width = solved.shape[1] - rank * level
        blocks[level][...] = gram[rank * level : rank * (level + 1), :width]


def level_kernel(rank, count, current, coupling_ref, *refs):
    own, other = refs[:count], refs[count : 2 * count]
    coef_ref, rest = refs[2 * count], refs[2 * count + 1 : 3 * count]
    pair_ref = refs[3 * count]
    front = own[0][...] + other[0][...]
    width = front.shape[1] - rank
    eye = identity(rank)
    gram = front[:, width:]
    extra = 1.0 / coupling_ref[current : current + 1, :]
    capacity = 0.5 * (gram + gram.T) + eye * extra
    diag_row = jnp.sum(capacity * eye, axis=0, keepdims=True)
    diag_col = jnp.sum(capacity * eye, axis=1, keepdims=True)
    root_row, root_col = lax.rsqrt(diag_row), lax.rsqrt(diag_col)
    scaled = capacity * root_row * root_col
    low = 0.99 * jnp.min(extra / diag_row)
    high = jnp.max(jnp.sum(jnp.abs(scaled), axis=0, keepdims=True))
    inverse = spd_inverse(scaled, low, high, pair_ref)
    projected = front[:, :width]
    coef = root_col * mm(inverse, root_col * projected)
    coef_ref[...] = coef
    if count > 1:
        base = width - rank * (count - 1)
        update = mm_t(projected[:, base:], coef)
        for index in range(1, count):
            rows = rank * (count - 1 - index)
            wide = own[index].shape[1]
            rest[index - 1][...] = (
                own[index][...] + other[index][...]
            ) - update[rows : rows + rank, :wide]


def from_partner(value, axis, distance):
    mask = 2**distance
    pairs = [(source, source ^ mask) for source in range(lax.axis_size(axis))]
    return lax.ppermute(value, axis, pairs)


def per_device(leaf_blocks, bases, targets, coupling):
    levels, rank = coupling.shape
    rows, size = leaf_blocks.shape
    width = targets.shape[1] + rank * levels
    inner_bits = lax.axis_size("inner").bit_length() - 1
    f32 = jnp.float32
    widths = [width - rank * level for level in range(levels)]
    solved, *blocks = pl.pallas_call(
        functools.partial(leaf_kernel, rank, levels),
        out_shape=[jax.ShapeDtypeStruct((rows, width), f32)]
        + [jax.ShapeDtypeStruct((rank, wide), f32) for wide in widths],
        in_specs=[VMEM] * 3,
        out_specs=[VMEM] * (1 + levels),
        scratch_shapes=[pltpu.VMEM((2 * size, size), f32)],
        compiler_params=pltpu.CompilerParams(vmem_limit_bytes=32 * 2**20),
        name="leaf",
    )(leaf_blocks, bases, targets)
    for current in range(levels):
        if current < inner_bits:
            axis, bit = "inner", current
        else:
            axis, bit = "group", current - inner_bits
        others = [from_partner(block, axis, bit) for block in blocks]
        count = levels - current
        wide = widths[current] - rank
        coef, *blocks = pl.pallas_call(
            functools.partial(level_kernel, rank, count, current),
            out_shape=[jax.ShapeDtypeStruct((rank, wide), f32)]
            + [jax.ShapeDtypeStruct(block.shape, f32) for block in blocks[1:]],
            in_specs=[VMEM] * (1 + 2 * count),
            out_specs=[VMEM] * count,
            scratch_shapes=[pltpu.VMEM((2 * rank, rank), f32)],
            compiler_params=pltpu.CompilerParams(vmem_limit_bytes=32 * 2**20),
            name="level",
        )(coupling, *blocks, *others)
        solved = solved[:, :wide] - mm(solved[:, wide:], coef)
    return solved


def solution(mesh):
    rows = P(("group", "inner"), None)
    return jax.shard_map(
        per_device,
        mesh=mesh,
        in_specs=(rows, rows, rows, P()),
        out_specs=rows,
        check_vma=False,
    )
```

time: 176 us -> 55.1 us (0.31)
  other arithmetic: 115 us -> 0 us
  Pallas kernels: 0 us -> 16.8 us
  waiting for transfers between devices: 31.6 us -> 17.6 us
  matrix products: 10.4 us -> 2.67 us
  starting transfers between devices: 9 us -> 16.6 us
  local copies, waits for them, and re-layouts: 7.7 us -> 1.2 us
    another operation x34 -> x0, other arithmetic: 114 us -> none  [the longest x13 47.8 us: chol_solve(): lax.linalg.triangular_solve(factor, forward, left_side=True, lower=True,...]
    pallas_call x0 -> x6, Pallas kernels: none -> 16.8 us  [the longest x5 11.3 us: per_device(): pl.pallas_call(functools.partial(level_kernel, rank, count, current), out...]
    ppermute x5 -> x15, waiting for transfers between devices: 31.6 us -> 17.6 us  [from_partner(): return lax.ppermute(value, axis, pairs)]
    ppermute x5 -> x15, starting transfers between devices: 9 us -> 16.6 us  [from_partner(): return lax.ppermute(value, axis, pairs)]
    another operation x18 -> x0, matrix products: 5.6 us -> none  [the longest x8 2.88 us: chol_solve(): lax.linalg.triangular_solve(factor, rhs_cols, left_side=True, lower=True)]
    another operation x9 -> x0, local copies, waits for them, and re-layouts: 4.12 us -> none
    dot_general x10 -> x5, matrix products: 4.84 us -> 2.67 us  [mm(): jnp.dot(first, second, precision=lax.Precision.HIGHEST, preferred_element...]
  transfers between devices with their start and end apart: 5 -> 15, of which waited for: 5 -> 7; matrix products, arithmetic and copies ran while one was open for 1% -> 3% of each run, Pallas kernels for 0% -> 0%
where the time goes in v1:
time: 55.1 us; the launch traced here: 55 us
  waiting for transfers between devices  17.6 us (32%)
  Pallas kernels  16.8 us (30%)
  starting transfers between devices  16.6 us (30%)
  matrix products  2.67 us (5%)
  local copies, waits for them, and re-layouts  1.2 us (2%)
    ppermute x15, waiting for transfers between devices, from_partner(): return lax.ppermute(value, axis, pairs)  17.6 us
    ppermute x15, starting transfers between devices, from_partner(): return lax.ppermute(value, axis, pairs)  16.6 us
    pallas_call x5, Pallas kernels, per_device(): pl.pallas_call(functools.partial(level_kernel, rank, count, current), out...  11.3 us
    pallas_call x1, Pallas kernels, per_device(): pl.pallas_call(functools.partial(leaf_kernel, rank, levels), out_shape=[j...  5.49 us
    dot_general x5, matrix products, mm(): jnp.dot(first, second, precision=lax.Precision.HIGHEST, preferred_element...  2.67 us
    unnamed x7, local copies, waits for them, and re-layouts  1.2 us
  transfers between devices with their start and end apart: 15, of which 7 were waited for; matrix products, arithmetic and copies ran while one was open for 3% of the time, Pallas kernels for 0%

profile of v1, /device:TPU:0, one launch (start us, length us, event | category | flops | bytes accessed | tf_op | source)
XLA Modules:
  0.0 55.0 jit_solution(6796349189485141080)
XLA Ops:
  0.0 0.0 copy-start.1
  0.0 0.0 copy-start
  0.0 1.2 %copy.5.bases_ref = f32[256,320]{1,0:T(8,128)S(1)} copy(f32[256,320]{0,1:T(8,128)} %param.5) | data formatting | bytes 655360 | tf_op args[1]
  1.2 0.0 copy-done.1
  1.2 0.0 copy-done
  1.2 5.5 %leaf.1 = (f32[256,448]{1,0:T(8,128)S(1)}, f32[64,448]{1,0:T(8,128)S(1)}, f32[64,384]{1,0:T(8,128)S(1)}, f32[64,320]{1,0:T(8,128)S(1)}, f32[64,256]{1,0:T(8,128)S(1)}, /*index=5*/f32[64,192]{1,0:T(8,128)S(1)}) custom-call(f32[256,256]{1,0:T(8,128)S(1)} %copy-done, f32[256,320]{1,0:T(8,128)S(1)} %copy.5.bases_ref, f32[256,128]{1,0:T(8,128)S(1)} %copy-done.1), custom_call_target="tpu_custom_call" | custom-call | tf_op jit(solution)/shard_map/leaf/pallas_call | solution.py:126
  6.7 0.0 copy-start.2
  6.7 3.0 %collective-permute-start = (f32[64,448]{1,0:T(8,128)S(1)}, f32[64,448]{1,0:T(8,128)S(1)}, u32[]{:S(2)}, u32[]{:S(2)}) collective-permute-start(f32[64,448]{1,0:T(8,128)S(1)} %get-tuple-element.26.refs_0_), channel_id=1, source_target_pairs={{0,1},{1,0},{2,3},{3,2},{4,5},{5,4},{6,7},{7,6},{8,9},{9,8},{10,11... | collective-permute-start | bytes 344072 | tf_op jit(solution)/shard_map/ppermute | solution.py:116
  9.7 0.1 collective-permute-start.1
  9.8 1.9 %collective-permute-start.2 = (f32[64,320]{1,0:T(8,128)S(1)}, f32[64,320]{1,0:T(8,128)S(1)}, u32[]{:S(2)}, u32[]{:S(2)}) collective-permute-start(f32[64,320]{1,0:T(8,128)S(1)} %get-tuple-element.28.refs_2_), channel_id=1, source_target_pairs={{0,1},{1,0},{2,3},{3,2},{4,5},{5,4},{6,7},{7,6},{8,9},{9,8},{10,11... | collective-permute-start | bytes 245768 | tf_op jit(solution)/shard_map/ppermute | solution.py:116
  11.8 0.1 collective-permute-start.3
  11.8 1.9 %collective-permute-start.4 = (f32[64,192]{1,0:T(8,128)S(1)}, f32[64,192]{1,0:T(8,128)S(1)}, u32[]{:S(2)}, u32[]{:S(2)}) collective-permute-start(f32[64,192]{1,0:T(8,128)S(1)} %get-tuple-element.30.refs_4_), channel_id=1, source_target_pairs={{0,1},{1,0},{2,3},{3,2},{4,5},{5,4},{6,7},{7,6},{8,9},{9,8},{10,11... | collective-permute-start | bytes 147464 | tf_op jit(solution)/shard_map/ppermute | solution.py:116
  13.8 6.5 %collective-permute-done.4.refs_9_ = f32[64,192]{1,0:T(8,128)S(1)} collective-permute-done((f32[64,192]{1,0:T(8,128)S(1)}, f32[64,192]{1,0:T(8,128)S(1)}, u32[]{:S(2)}, u32[]{:S(2)}) %collective-permute-start.4) | collective-permute-done | bytes 49184 | tf_op jit(solution)/shard_map/ppermute | solution.py:116
  20.2 0.0 collective-permute-done.3.refs_8_
  20.3 0.0 collective-permute-done.2.refs_7_
  20.3 0.0 collective-permute-done.1.refs_6_
  20.3 0.0 collective-permute-done.refs_5_
  20.3 0.0 copy-done.2
  20.3 2.0 %level.5 = (f32[64,384]{1,0:T(8,128)S(1)}, f32[64,384]{1,0:T(8,128)S(1)}, f32[64,320]{1,0:T(8,128)S(1)}, f32[64,256]{1,0:T(8,128)S(1)}, f32[64,192]{1,0:T(8,128)S(1)}) custom-call(f32[5,64]{1,0:T(8,128)S(1)} %copy-done.2, f32[64,448]{1,0:T(8,128)S(1)} %get-tuple-element.26.refs_0_, f32[64,384]{1,0:T(8,128)S(1)} %get-tuple-element.27.refs_1_, ...), custom_call_target="tpu_custom_call" | custom-call | tf_op jit(solution)/shard_map/level/pallas_call | solution.py:144
  22.3 1.8 %collective-permute-start.7 = (f32[64,256]{1,0:T(8,128)S(1)}, f32[64,256]{1,0:T(8,128)S(1)}, u32[]{:S(2)}, u32[]{:S(2)}) collective-permute-start(f32[64,256]{1,0:T(8,128)S(1)} %get-tuple-element.34.refs_2_), channel_id=1, source_target_pairs={{0,2},{1,3},{2,0},{3,1},{4,6},{5,7},{6,4},{7,5},{8,10},{9,11},{10,... | collective-permute-start | bytes 196616 | tf_op jit(solution)/shard_map/ppermute | solution.py:116
  24.1 0.3 collective-permute-start.8
  24.4 1.8 %collective-permute-start.5 = (f32[64,384]{1,0:T(8,128)S(1)}, f32[64,384]{1,0:T(8,128)S(1)}, u32[]{:S(2)}, u32[]{:S(2)}) collective-permute-start(f32[64,384]{1,0:T(8,128)S(1)} %get-tuple-element.32.refs_0_), channel_id=1, source_target_pairs={{0,2},{1,3},{2,0},{3,1},{4,6},{5,7},{6,4},{7,5},{8,10},{9,11},{10,... | collective-permute-start | bytes 294920 | tf_op jit(solution)/shard_map/ppermute | solution.py:116
  26.2 0.3 collective-permute-start.6
  26.4 0.5 convolution_subtract_fusion
  26.9 2.3 %collective-permute-done.8.refs_7_ = f32[64,192]{1,0:T(8,128)S(1)} collective-permute-done((f32[64,192]{1,0:T(8,128)S(1)}, f32[64,192]{1,0:T(8,128)S(1)}, u32[]{:S(2)}, u32[]{:S(2)}) %collective-permute-start.8) | collective-permute-done | bytes 49184 | tf_op jit(solution)/shard_map/ppermute | solution.py:116
  29.2 0.0 collective-permute-done.7.refs_6_
  29.2 2.6 %collective-permute-done.6.refs_5_ = f32[64,320]{1,0:T(8,128)S(1)} collective-permute-done((f32[64,320]{1,0:T(8,128)S(1)}, f32[64,320]{1,0:T(8,128)S(1)}, u32[]{:S(2)}, u32[]{:S(2)}) %collective-permute-start.6) | collective-permute-done | bytes 81952 | tf_op jit(solution)/shard_map/ppermute | solution.py:116
  31.7 0.0 collective-permute-done.5.refs_4_
  31.7 2.6 %level.6 = (f32[64,320]{1,0:T(8,128)S(1)}, f32[64,320]{1,0:T(8,128)S(1)}, f32[64,256]{1,0:T(8,128)S(1)}, f32[64,192]{1,0:T(8,128)S(1)}) custom-call(f32[5,64]{1,0:T(8,128)S(1)} %copy-done.2, f32[64,384]{1,0:T(8,128)S(1)} %get-tuple-element.32.refs_0_, f32[64,320]{1,0:T(8,128)S(1)} %get-tuple-element.33.refs_1_, f32[64,256]{1,0:T(8,128)S(1)} %get-tuple-element.34.refs_2_, ...), custom_call_target="tpu_custom_call" | custom-call | tf_op jit(solution)/shard_map/level/pallas_call | solution.py:144
  34.4 0.1 collective-permute-start.10
  34.5 0.5 collective-permute-start.11
  35.0 0.1 collective-permute-start.9
  35.0 0.5 slice_subtract_fusion
  35.6 0.3 collective-permute-done.11.refs_5_
  35.9 0.0 collective-permute-done.10.refs_4_
  35.9 0.4 collective-permute-done.9.refs_3_
  36.3 2.2 %level.7 = (f32[64,256]{1,0:T(8,128)S(1)}, f32[64,256]{1,0:T(8,128)S(1)}, f32[64,192]{1,0:T(8,128)S(1)}) custom-call(f32[5,64]{1,0:T(8,128)S(1)} %copy-done.2, f32[64,320]{1,0:T(8,128)S(1)} %get-tuple-element.37.refs_0_, f32[64,256]{1,0:T(8,128)S(1)} %get-tuple-element.38.refs_1_, f32[64,192]{1,0:T(8,128)S(1)} %get-tuple-element.39.refs_2_, ...), custom_call_target="tpu_custom_call" | custom-call | tf_op jit(solution)/shard_map/level/pallas_call | solution.py:144
  38.4 1.6 %collective-permute-start.12 = (f32[64,256]{1,0:T(8,128)S(1)}, f32[64,256]{1,0:T(8,128)S(1)}, u32[]{:S(2)}, u32[]{:S(2)}) collective-permute-start(f32[64,256]{1,0:T(8,128)S(1)} %get-tuple-element.41.refs_0_), channel_id=1, source_target_pairs={{0,8},{4,12},{8,0},{12,4},{16,24},{20,28},{24,16},{28,20},{1,9},{5... | collective-permute-start | bytes 196616 | tf_op jit(solution)/shard_map/ppermute | solution.py:116
  40.1 0.4 collective-permute-start.13
  40.5 0.3 slice_subtract_fusion.2
  40.9 3.5 %collective-permute-done.13.refs_3_ = f32[64,192]{1,0:T(8,128)S(1)} collective-permute-done((f32[64,192]{1,0:T(8,128)S(1)}, f32[64,192]{1,0:T(8,128)S(1)}, u32[]{:S(2)}, u32[]{:S(2)}) %collective-permute-start.13) | collective-permute-done | bytes 49184 | tf_op jit(solution)/shard_map/ppermute | solution.py:116
  44.4 0.0 collective-permute-done.12.refs_2_
  44.4 2.4 %level.8 = (f32[64,192]{1,0:T(8,128)S(1)}, f32[64,192]{1,0:T(8,128)S(1)}) custom-call(f32[5,64]{1,0:T(8,128)S(1)} %copy-done.2, f32[64,256]{1,0:T(8,128)S(1)} %get-tuple-element.41.refs_0_, f32[64,192]{1,0:T(8,128)S(1)} %get-tuple-element.42.refs_1_, f32[64,256]{1,0:T(8,128)S(1)} %collective-permute-done.12.refs_2_, ...), custom_call_target="tpu_custom_call" | custom-call | tf_op jit(solution)/shard_map/level/pallas_call | solution.py:144
  46.8 2.7 %collective-permute-start.14 = (f32[64,192]{1,0:T(8,128)S(1)}, f32[64,192]{1,0:T(8,128)S(1)}, u32[]{:S(2)}, u32[]{:S(2)}) collective-permute-start(f32[64,192]{1,0:T(8,128)S(1)} %get-tuple-element.44.refs_0_), channel_id=1, source_target_pairs={{0,16},{4,20},{8,24},{12,28},{16,0},{20,4},{24,8},{28,12},{1,17},{... | collective-permute-start | bytes 147464 | tf_op jit(solution)/shard_map/ppermute | solution.py:116
  49.5 0.4 slice_subtract_fusion.1
  49.9 2.1 %collective-permute-done.14.refs_1_ = f32[64,192]{1,0:T(8,128)S(1)} collective-permute-done((f32[64,192]{1,0:T(8,128)S(1)}, f32[64,192]{1,0:T(8,128)S(1)}, u32[]{:S(2)}, u32[]{:S(2)}) %collective-permute-start.14) | collective-permute-done | bytes 49184 | tf_op jit(solution)/shard_map/ppermute | solution.py:116
  52.0 2.0 %level.9 = f32[64,128]{1,0:T(8,128)S(1)} custom-call(f32[5,64]{1,0:T(8,128)S(1)} %copy-done.2, f32[64,192]{1,0:T(8,128)S(1)} %get-tuple-element.44.refs_0_, f32[64,192]{1,0:T(8,128)S(1)} %collective-permute-done.14.refs_1_), custom_call_target="tpu_custom_call" | custom-call | tf_op jit(solution)/shard_map/level/pallas_call | solution.py:144
  54.0 0.9 %slice_subtract_fusion.3 = f32[256,128]{1,0:T(8,128)} fusion(f32[256,192]{1,0:T(8,128)S(1)} %slice_subtract_fusion.1, f32[64,128]{1,0:T(8,128)S(1)} %level.9), kind=kOutput, calls=%fused_computation.6 | convolution fusion | flops 25198592 | bytes 360448 | tf_op jit(solution)/shard_map/dot_general | solution.py:16
Async XLA Ops:
  0.0 1.2 %copy-start.1 = (f32[256,128]{1,0:T(8,128)S(1)}, f32[256,128]{1,0:T(8,128)}, u32[]{:S(2)}) copy-start(f32[256,128]{1,0:T(8,128)} %targets_ref.1) | copy-start | bytes 393220
  0.0 1.2 %copy-start = (f32[256,256]{1,0:T(8,128)S(1)}, f32[256,256]{1,0:T(8,128)}, u32[]{:S(2)}) copy-start(f32[256,256]{1,0:T(8,128)} %leaf_ref.1) | copy-start | bytes 786436
  6.7 13.6 %copy-start.2 = (f32[5,64]{1,0:T(8,128)S(1)}, f32[5,64]{1,0:T(8,128)}, u32[]{:S(2)}) copy-start(f32[5,64]{1,0:T(8,128)} %coupling_ref.9) | copy-start | bytes 3844
  6.7 13.5 %collective-permute-start = (f32[64,448]{1,0:T(8,128)S(1)}, f32[64,448]{1,0:T(8,128)S(1)}, u32[]{:S(2)}, u32[]{:S(2)}) collective-permute-start(f32[64,448]{1,0:T(8,128)S(1)} %get-tuple-element.26.refs_0_), channel_id=1, source_target_pairs={{0,1},{1,0},{2,3},{3,2},{4,5},{5,4},{6,7},{7,6},{8,9},{9,8},{10,11... | collective-permute-start | bytes 344072 | tf_op jit(solution)/shard_map/ppermute | solution.py:116
  9.7 10.5 %collective-permute-start.1 = (f32[64,384]{1,0:T(8,128)S(1)}, f32[64,384]{1,0:T(8,128)S(1)}, u32[]{:S(2)}, u32[]{:S(2)}) collective-permute-start(f32[64,384]{1,0:T(8,128)S(1)} %get-tuple-element.27.refs_1_), channel_id=1, source_target_pairs={{0,1},{1,0},{2,3},{3,2},{4,5},{5,4},{6,7},{7,6},{8,9},{9,8},{10,11... | collective-permute-start | bytes 294920 | tf_op jit(solution)/shard_map/ppermute | solution.py:116
  9.8 10.4 %collective-permute-start.2 = (f32[64,320]{1,0:T(8,128)S(1)}, f32[64,320]{1,0:T(8,128)S(1)}, u32[]{:S(2)}, u32[]{:S(2)}) collective-permute-start(f32[64,320]{1,0:T(8,128)S(1)} %get-tuple-element.28.refs_2_), channel_id=1, source_target_pairs={{0,1},{1,0},{2,3},{3,2},{4,5},{5,4},{6,7},{7,6},{8,9},{9,8},{10,11... | collective-permute-start | bytes 245768 | tf_op jit(solution)/shard_map/ppermute | solution.py:116
  11.8 8.5 %collective-permute-start.3 = (f32[64,256]{1,0:T(8,128)S(1)}, f32[64,256]{1,0:T(8,128)S(1)}, u32[]{:S(2)}, u32[]{:S(2)}) collective-permute-start(f32[64,256]{1,0:T(8,128)S(1)} %get-tuple-element.29.refs_3_), channel_id=1, source_target_pairs={{0,1},{1,0},{2,3},{3,2},{4,5},{5,4},{6,7},{7,6},{8,9},{9,8},{10,11... | collective-permute-start | bytes 196616 | tf_op jit(solution)/shard_map/ppermute | solution.py:116
  11.8 8.4 %collective-permute-start.4 = (f32[64,192]{1,0:T(8,128)S(1)}, f32[64,192]{1,0:T(8,128)S(1)}, u32[]{:S(2)}, u32[]{:S(2)}) collective-permute-start(f32[64,192]{1,0:T(8,128)S(1)} %get-tuple-element.30.refs_4_), channel_id=1, source_target_pairs={{0,1},{1,0},{2,3},{3,2},{4,5},{5,4},{6,7},{7,6},{8,9},{9,8},{10,11... | collective-permute-start | bytes 147464 | tf_op jit(solution)/shard_map/ppermute | solution.py:116
  22.3 6.9 %collective-permute-start.7 = (f32[64,256]{1,0:T(8,128)S(1)}, f32[64,256]{1,0:T(8,128)S(1)}, u32[]{:S(2)}, u32[]{:S(2)}) collective-permute-start(f32[64,256]{1,0:T(8,128)S(1)} %get-tuple-element.34.refs_2_), channel_id=1, source_target_pairs={{0,2},{1,3},{2,0},{3,1},{4,6},{5,7},{6,4},{7,5},{8,10},{9,11},{10,... | collective-permute-start | bytes 196616 | tf_op jit(solution)/shard_map/ppermute | solution.py:116
  24.1 5.0 %collective-permute-start.8 = (f32[64,192]{1,0:T(8,128)S(1)}, f32[64,192]{1,0:T(8,128)S(1)}, u32[]{:S(2)}, u32[]{:S(2)}) collective-permute-start(f32[64,192]{1,0:T(8,128)S(1)} %get-tuple-element.35.refs_3_), channel_id=1, source_target_pairs={{0,2},{1,3},{2,0},{3,1},{4,6},{5,7},{6,4},{7,5},{8,10},{9,11},{10,... | collective-permute-start | bytes 147464 | tf_op jit(solution)/shard_map/ppermute | solution.py:116
  24.4 7.3 %collective-permute-start.5 = (f32[64,384]{1,0:T(8,128)S(1)}, f32[64,384]{1,0:T(8,128)S(1)}, u32[]{:S(2)}, u32[]{:S(2)}) collective-permute-start(f32[64,384]{1,0:T(8,128)S(1)} %get-tuple-element.32.refs_0_), channel_id=1, source_target_pairs={{0,2},{1,3},{2,0},{3,1},{4,6},{5,7},{6,4},{7,5},{8,10},{9,11},{10,... | collective-permute-start | bytes 294920 | tf_op jit(solution)/shard_map/ppermute | solution.py:116
  26.2 5.6 %collective-permute-start.6 = (f32[64,320]{1,0:T(8,128)S(1)}, f32[64,320]{1,0:T(8,128)S(1)}, u32[]{:S(2)}, u32[]{:S(2)}) collective-permute-start(f32[64,320]{1,0:T(8,128)S(1)} %get-tuple-element.33.refs_1_), channel_id=1, source_target_pairs={{0,2},{1,3},{2,0},{3,1},{4,6},{5,7},{6,4},{7,5},{8,10},{9,11},{10,... | collective-permute-start | bytes 245768 | tf_op jit(solution)/shard_map/ppermute | solution.py:116
  34.4 1.5 %collective-permute-start.10 = (f32[64,256]{1,0:T(8,128)S(1)}, f32[64,256]{1,0:T(8,128)S(1)}, u32[]{:S(2)}, u32[]{:S(2)}) collective-permute-start(f32[64,256]{1,0:T(8,128)S(1)} %get-tuple-element.38.refs_1_), channel_id=1, source_target_pairs={{0,4},{4,0},{8,12},{12,8},{16,20},{20,16},{24,28},{28,24},{1,5},{5... | collective-permute-start | bytes 196616 | tf_op jit(solution)/shard_map/ppermute | solution.py:116
  34.5 1.4 %collective-permute-start.11 = (f32[64,192]{1,0:T(8,128)S(1)}, f32[64,192]{1,0:T(8,128)S(1)}, u32[]{:S(2)}, u32[]{:S(2)}) collective-permute-start(f32[64,192]{1,0:T(8,128)S(1)} %get-tuple-element.39.refs_2_), channel_id=1, source_target_pairs={{0,4},{4,0},{8,12},{12,8},{16,20},{20,16},{24,28},{28,24},{1,5},{5... | collective-permute-start | bytes 147464 | tf_op jit(solution)/shard_map/ppermute | solution.py:116
  35.0 1.3 %collective-permute-start.9 = (f32[64,320]{1,0:T(8,128)S(1)}, f32[64,320]{1,0:T(8,128)S(1)}, u32[]{:S(2)}, u32[]{:S(2)}) collective-permute-start(f32[64,320]{1,0:T(8,128)S(1)} %get-tuple-element.37.refs_0_), channel_id=1, source_target_pairs={{0,4},{4,0},{8,12},{12,8},{16,20},{20,16},{24,28},{28,24},{1,5},{5... | collective-permute-start | bytes 245768 | tf_op jit(solution)/shard_map/ppermute | solution.py:116
  38.4 5.9 %collective-permute-start.12 = (f32[64,256]{1,0:T(8,128)S(1)}, f32[64,256]{1,0:T(8,128)S(1)}, u32[]{:S(2)}, u32[]{:S(2)}) collective-permute-start(f32[64,256]{1,0:T(8,128)S(1)} %get-tuple-element.41.refs_0_), channel_id=1, source_target_pairs={{0,8},{4,12},{8,0},{12,4},{16,24},{20,28},{24,16},{28,20},{1,9},{5... | collective-permute-start | bytes 196616 | tf_op jit(solution)/shard_map/ppermute | solution.py:116
  40.1 4.3 %collective-permute-start.13 = (f32[64,192]{1,0:T(8,128)S(1)}, f32[64,192]{1,0:T(8,128)S(1)}, u32[]{:S(2)}, u32[]{:S(2)}) collective-permute-start(f32[64,192]{1,0:T(8,128)S(1)} %get-tuple-element.42.refs_1_), channel_id=1, source_target_pairs={{0,8},{4,12},{8,0},{12,4},{16,24},{20,28},{24,16},{28,20},{1,9},{5... | collective-permute-start | bytes 147464 | tf_op jit(solution)/shard_map/ppermute | solution.py:116
  46.8 5.2 %collective-permute-start.14 = (f32[64,192]{1,0:T(8,128)S(1)}, f32[64,192]{1,0:T(8,128)S(1)}, u32[]{:S(2)}, u32[]{:S(2)}) collective-permute-start(f32[64,192]{1,0:T(8,128)S(1)} %get-tuple-element.44.refs_0_), channel_id=1, source_target_pairs={{0,16},{4,20},{8,24},{12,28},{16,0},{20,4},{24,8},{28,12},{1,17},{... | collective-permute-start | bytes 147464 | tf_op jit(solution)/shard_map/ppermute | solution.py:116

commit v2 on v1

v2 whole, which is shorter than its diff:
```python
import functools
import math

import jax
import jax.numpy as jnp
from jax import lax
from jax.experimental import pallas as pl
from jax.experimental.pallas import tpu as pltpu
from jax.sharding import PartitionSpec as P

EIGEN_MIN = 0.4
LEAF_TOL = 3e-4
VMEM = pl.BlockSpec(memory_space=pltpu.VMEM)


def mm(first, second):
    return jnp.dot(
        first,
        second,
        precision=lax.Precision.HIGHEST,
        preferred_element_type=jnp.float32,
    )


def mm_t(first, second):
    return lax.dot_general(
        first,
        second,
        (((0,), (0,)), ((), ())),
        precision=lax.Precision.HIGHEST,
        preferred_element_type=jnp.float32,
    )


def mm_nt(first, second):
    return lax.dot_general(
        first,
        second,
        (((1,), (1,)), ((), ())),
        precision=lax.Precision.HIGHEST,
        preferred_element_type=jnp.float32,
    )


def identity(size):
    rows = lax.broadcasted_iota(jnp.int32, (size, size), 0)
    cols = lax.broadcasted_iota(jnp.int32, (size, size), 1)
    return jnp.where(rows == cols, 1.0, 0.0).astype(jnp.float32)


def spd_inverse(matrix, low, high, pair_ref):
    size = matrix.shape[0]
    eye = identity(size)
    alpha = 2.0 / (low + high)
    pair_ref[:size, :] = eye - alpha * matrix
    pair_ref[size:, :] = alpha * eye

    def cond(rho):
        return rho > LEAF_TOL

    def body(rho):
        square = rho * rho
        scale = 2.0 / (2.0 - square)
        pair = pair_ref[...]
        product = mm(pair, pair[:size])
        pair_ref[:size, :] = (1.0 - scale) * eye + scale * product[:size]
        pair_ref[size:, :] = scale * (pair[size:] + product[size:])
        return square / (2.0 - square)

    lax.while_loop(cond, body, (high - low) / (high + low))
    inverse = pair_ref[size:, :]
    return inverse + mm(inverse, eye - mm(matrix, inverse))


def leaf_kernel(rank, levels, leaf_ref, bases_ref, targets_ref, solved_ref, *rest):
    blocks, pair_ref = rest[:levels], rest[levels]
    matrix = leaf_ref[...]
    high = jnp.max(jnp.sum(jnp.abs(matrix), axis=0, keepdims=True))
    inverse = spd_inverse(matrix, EIGEN_MIN, jnp.maximum(high, 2 * EIGEN_MIN), pair_ref)
    flipped = jnp.concatenate(
        [
            bases_ref[rank * level : rank * (level + 1), :]
            for level in reversed(range(levels))
        ],
        axis=0,
    )
    solved = jnp.concatenate(
        [mm(inverse, targets_ref[...]), mm_nt(inverse, flipped)], axis=1
    )
    solved_ref[...] = solved
    gram = mm(bases_ref[...], solved)
    for level in range(levels):
        width = solved.shape[1] - rank * level
        blocks[level][...] = gram[rank * level : rank * (level + 1), :width]


def fixed_inverse(matrix, low, high, doublings):
    size = matrix.shape[0]
    eye = identity(size)
    alpha = 2.0 / (low + high)
    rho = (high - low) / (high + low)
    residual = eye - alpha * matrix
    inverse = alpha * eye
    for _ in range(doublings):
        square = rho * rho
        scale = 2.0 / (2.0 - square)
        rho = square / (2.0 - square)
        product = mm(jnp.concatenate([residual, inverse], axis=0), residual)
        inverse = scale * (inverse + product[size:])
        residual = (1.0 - scale) * eye + scale * product[:size]
    return inverse + mm(inverse, eye - mm(matrix, inverse))


def capacity_solve(front, weights, rank, doublings):
    width = front.shape[1] - rank
    eye = identity(rank)
    gram = front[:, width:]
    extra = 1.0 / weights
    capacity = 0.5 * (gram + gram.T) + eye * extra
    diag_row = jnp.sum(capacity * eye, axis=0, keepdims=True)
    diag_col = jnp.sum(capacity * eye, axis=1, keepdims=True)
    root_row, root_col = lax.rsqrt(diag_row), lax.rsqrt(diag_col)
    scaled = capacity * root_row * root_col
    low = 0.99 * jnp.min(extra / diag_row, axis=1, keepdims=True)
    sums = jnp.sum(jnp.abs(scaled), axis=0, keepdims=True)
    high = jnp.max(sums, axis=1, keepdims=True)
    low = jnp.broadcast_to(low, (1, rank))
    high = jnp.broadcast_to(high, (1, rank))
    inverse = fixed_inverse(scaled, low, high, doublings)
    return root_col * mm(inverse, root_col * front[:, :width])


def tree_kernel(rank, levels, inner_bits, doublings, coupling_ref, solved_ref, *refs):
    pairs = [(k, j) for k in range(levels) for j in range(k, levels)]
    number = {pair: index for index, pair in enumerate(pairs)}
    first, refs = refs[:levels], refs[levels:]
    out_ref, state_ref, refs = refs[0], refs[1], refs[2:]
    landed = dict(zip(pairs, refs[: len(pairs)]))
    later = pairs[levels:]
    own = dict(zip(pairs[:levels], first))
    own.update(zip(later, refs[len(pairs) : len(pairs) + len(later)]))
    send_sem, recv_sem = refs[-2:]

    group, inner = lax.axis_index("group"), lax.axis_index("inner")

    def partner(level):
        if level < inner_bits:
            mask = 2**level
            return (group, inner + mask * (1 - 2 * ((inner // mask) % 2)))
        mask = 2 ** (level - inner_bits)
        return (group + mask * (1 - 2 * ((group // mask) % 2)), inner)

    partners = [partner(level) for level in range(levels)]

    def copy_of(k, j):
        return pltpu.make_async_remote_copy(
            src_ref=own[k, j],
            dst_ref=landed[k, j],
            send_sem=send_sem.at[number[k, j]],
            recv_sem=recv_sem.at[number[k, j]],
            device_id=partners[k],
            device_id_type=pl.DeviceIdType.MESH,
        )

    barrier = pltpu.get_barrier_semaphore()
    for other in partners:
        pl.semaphore_signal(
            barrier, inc=1, device_id=other, device_id_type=pl.DeviceIdType.MESH
        )
    pl.semaphore_wait(barrier, levels)

    for j in range(levels):
        copy_of(0, j).start()
    state_ref[...] = solved_ref[...]
    for k in range(levels):
        copy_of(k, k).wait_recv()
        front = own[k, k][...] + landed[k, k][...]
        wide = front.shape[1] - rank
        coef = capacity_solve(front, coupling_ref[k : k + 1, :], rank, doublings)
        if k + 1 < levels:
            base = wide - rank * (levels - 1 - k)
            update = mm_t(front[:, base:wide], coef)
            for j in range(k + 1, levels):
                rows = rank * (levels - 1 - j)
                columns = own[k, j].shape[1]
                copy_of(k, j).wait_recv()
                own[k + 1, j][...] = (own[k, j][...] + landed[k, j][...]) - update[
                    rows : rows + rank, :columns
                ]
                copy_of(k + 1, j).start()
            state_ref[:, :wide] = state_ref[:, :wide] - mm(
                state_ref[:, wide : wide + rank], coef
            )
        else:
            out_ref[...] = state_ref[:, :wide] - mm(
                state_ref[:, wide : wide + rank], coef
            )
    for pair in pairs:
        copy_of(*pair).wait_send()


def per_device(leaf_blocks, bases, targets, coupling):
    levels, rank = coupling.shape
    rows, size = leaf_blocks.shape
    right = targets.shape[1]
    width = right + rank * levels
    inner_bits = lax.axis_size("inner").bit_length() - 1
    f32 = jnp.float32
    widths = [width - rank * level for level in range(levels)]
    solved, *blocks = pl.pallas_call(
        functools.partial(leaf_kernel, rank, levels),
        out_shape=[jax.ShapeDtypeStruct((rows, width), f32)]
        + [jax.ShapeDtypeStruct((rank, wide), f32) for wide in widths],
        in_specs=[VMEM] * 3,
        out_specs=[VMEM] * (1 + levels),
        scratch_shapes=[pltpu.VMEM((2 * size, size), f32)],
        compiler_params=pltpu.CompilerParams(vmem_limit_bytes=32 * 2**20),
        name="leaf",
    )(leaf_blocks, bases.T, targets)
    pairs = [(k, j) for k in range(levels) for j in range(k, levels)]
    landed = [pltpu.VMEM((rank, widths[j]), f32) for _, j in pairs]
    worst = rank * (4.0 * rows * 2**levels / EIGEN_MIN + 1.0)
    doublings = math.ceil(math.log2(math.sqrt(worst) * 4.1))
    return pl.pallas_call(
        functools.partial(tree_kernel, rank, levels, inner_bits, doublings),
        out_shape=jax.ShapeDtypeStruct((rows, right), f32),
        in_specs=[VMEM] * (2 + levels),
        out_specs=VMEM,
        scratch_shapes=[pltpu.VMEM((rows, width), f32)]
        + landed
        + landed[levels:]
        + [pltpu.SemaphoreType.DMA((len(pairs),))] * 2,
        compiler_params=pltpu.CompilerParams(
            collective_id=0, has_side_effects=True, vmem_limit_bytes=40 * 2**20
        ),
        name="tree",
    )(coupling, solved, *blocks)


def solution(mesh):
    rows = P(("group", "inner"), None)
    return jax.shard_map(
        per_device,
        mesh=mesh,
        in_specs=(rows, rows, rows, P()),
        out_specs=rows,
        check_vma=False,
    )
```

time: 55.1 us -> 56.3 us (1.022)
  Pallas kernels: 16.8 us -> 51.9 us
  waiting for transfers between devices: 17.6 us -> 0 us
  starting transfers between devices: 16.6 us -> 0 us
  local copies, waits for them, and re-layouts: 1.2 us -> 4.17 us
  matrix products: 2.67 us -> 0 us
    pallas_call x5 -> x1, Pallas kernels: 11.3 us -> 46.2 us  [per_device(): pl.pallas_call(functools.partial(tree_kernel, rank, levels, inner_bits, d...]
    ppermute x15 -> x0, waiting for transfers between devices: 17.6 us -> none  [from_partner(): return lax.ppermute(value, axis, pairs)]
    ppermute x15 -> x0, starting transfers between devices: 16.6 us -> none  [from_partner(): return lax.ppermute(value, axis, pairs)]
    unnamed x7 -> x9, local copies, waits for them, and re-layouts: 1.2 us -> 4.17 us
    dot_general x5 -> x0, matrix products: 2.67 us -> none  [mm(): jnp.dot(first, second, precision=lax.Precision.HIGHEST, preferred_element...]
  transfers between devices with their start and end apart: 15 -> 0, of which waited for: 7 -> 0; matrix products, arithmetic and copies ran while one was open for 3% -> 0% of each run, Pallas kernels for 0% -> 0%
where the time goes in v2:
time: 56.3 us; the launch traced here: 56.1 us
  Pallas kernels  51.9 us (92%)
  local copies, waits for them, and re-layouts  4.17 us (7%)
    pallas_call x1, Pallas kernels, per_device(): pl.pallas_call(functools.partial(tree_kernel, rank, levels, inner_bits, d...  46.2 us
    pallas_call x1, Pallas kernels, per_device(): pl.pallas_call(functools.partial(leaf_kernel, rank, levels), out_shape=[j...  5.64 us
    unnamed x9, local copies, waits for them, and re-layouts  4.17 us

profile of v2, /device:TPU:0, one launch (start us, length us, event | category | flops | bytes accessed | tf_op | source)
XLA Modules:
  0.0 56.1 jit_solution(16058570087507133195)
XLA Ops:
  0.0 0.0 copy-start
  0.0 1.0 %copy-done = f32[256,320]{0,1:T(8,128)S(1)} copy-done((f32[256,320]{0,1:T(8,128)S(1)}, f32[256,320]{0,1:T(8,128)}, u32[]{:S(2)}) %copy-start) | copy-done | bytes 327704
  1.0 0.0 copy-start.1
  1.0 0.9 %copy-done.1 = f32[256,256]{1,0:T(8,128)S(1)} copy-done((f32[256,256]{1,0:T(8,128)S(1)}, f32[256,256]{1,0:T(8,128)}, u32[]{:S(2)}) %copy-start.1) | copy-done | bytes 262168
  1.9 0.0 copy-start.2
  1.9 0.9 %copy-done.2 = f32[256,128]{1,0:T(8,128)S(1)} copy-done((f32[256,128]{1,0:T(8,128)S(1)}, f32[256,128]{1,0:T(8,128)}, u32[]{:S(2)}) %copy-start.2) | copy-done | bytes 131096
  2.8 5.6 %leaf.1 = (f32[256,448]{1,0:T(8,128)S(1)}, f32[64,448]{1,0:T(8,128)S(1)}, f32[64,384]{1,0:T(8,128)S(1)}, f32[64,320]{1,0:T(8,128)S(1)}, f32[64,256]{1,0:T(8,128)S(1)}, /*index=5*/f32[64,192]{1,0:T(8,128)S(1)}) custom-call(f32[256,256]{1,0:T(8,128)S(1)} %copy-done.1, f32[320,256]{1,0:T(8,128)S(1)} %bitcast.1, f32[256,128]{1,0:T(8,128)S(1)} %copy-done.2), custom_call_target="tpu_custom_call" | custom-call | tf_op jit(solution)/shard_map/leaf/pallas_call | solution.py:210
  8.5 0.0 copy-start.3
  8.5 0.7 %copy-done.3 = f32[5,64]{1,0:T(8,128)S(1)} copy-done((f32[5,64]{1,0:T(8,128)S(1)}, f32[5,64]{1,0:T(8,128)}, u32[]{:S(2)}) %copy-start.3) | copy-done | bytes 1304
  9.2 46.2 %tree.1 = f32[256,128]{1,0:T(8,128)S(1)} custom-call(f32[5,64]{1,0:T(8,128)S(1)} %copy-done.3, f32[256,448]{1,0:T(8,128)S(1)} %get-tuple-element.11.solved_ref, f32[64,448]{1,0:T(8,128)S(1)} %get-tuple-element.12.refs_0_, f32[64,384]{1,0:T(8,128)S(1)} %get-tuple-element.13.refs_1_, f32[64,320]{1,0:T(8,128)S(1)} %get-tuple-element.14.refs_2_, ...), custom_call_target="tpu_custom_call" | custom-call | tf_op jit(solution)/shard_map/tree/pallas_call | solution.py:224
  55.4 0.7 %copy.6 = f32[256,128]{1,0:T(8,128)} copy(f32[256,128]{1,0:T(8,128)S(1)} %tree.1) | data formatting | bytes 262144
Async XLA Ops:
  0.0 1.0 %copy-start = (f32[256,320]{0,1:T(8,128)S(1)}, f32[256,320]{0,1:T(8,128)}, u32[]{:S(2)}) copy-start(f32[256,320]{0,1:T(8,128)} %param.5) | copy-start | bytes 983044
  1.0 0.9 %copy-start.1 = (f32[256,256]{1,0:T(8,128)S(1)}, f32[256,256]{1,0:T(8,128)}, u32[]{:S(2)}) copy-start(f32[256,256]{1,0:T(8,128)} %leaf_ref.1) | copy-start | bytes 786436
  1.9 0.9 %copy-start.2 = (f32[256,128]{1,0:T(8,128)S(1)}, f32[256,128]{1,0:T(8,128)}, u32[]{:S(2)}) copy-start(f32[256,128]{1,0:T(8,128)} %targets_ref.1) | copy-start | bytes 393220
  8.5 0.7 %copy-start.3 = (f32[5,64]{1,0:T(8,128)S(1)}, f32[5,64]{1,0:T(8,128)}, u32[]{:S(2)}) copy-start(f32[5,64]{1,0:T(8,128)} %coupling_ref.1) | copy-start | bytes 3844

commit v3 on v2

--- a/solution.py
+++ b/solution.py
@@ -10,6 +10,8 @@
 
 EIGEN_MIN = 0.4
 LEAF_TOL = 3e-4
+RESIDUAL_MAX = 1e-3
+FLAG_ROWS = 8
 VMEM = pl.BlockSpec(memory_space=pltpu.VMEM)
 
 
@@ -20,6 +22,17 @@
         precision=lax.Precision.HIGHEST,
         preferred_element_type=jnp.float32,
     )
+
+
+def split(value):
+    high = value.astype(jnp.bfloat16)
+    return high, (value - high.astype(jnp.float32)).astype(jnp.bfloat16)
+
+
+def mm3(first, second):
+    (a_high, a_low), (b_high, b_low) = split(first), split(second)
+    dot = functools.partial(jnp.dot, preferred_element_type=jnp.float32)
+    return dot(a_high, b_high) + (dot(a_high, b_low) + dot(a_low, b_high))
 
 
 def mm_t(first, second):
@@ -62,14 +75,23 @@
         square = rho * rho
         scale = 2.0 / (2.0 - square)
         pair = pair_ref[...]
-        product = mm(pair, pair[:size])
+        product = mm3(pair, pair[:size])
         pair_ref[:size, :] = (1.0 - scale) * eye + scale * product[:size]
         pair_ref[size:, :] = scale * (pair[size:] + product[size:])
         return square / (2.0 - square)
 
     lax.while_loop(cond, body, (high - low) / (high + low))
-    inverse = pair_ref[size:, :]
-    return inverse + mm(inverse, eye - mm(matrix, inverse))
+    pair_ref[size:, :] = pair_ref[size:, :] + mm(
+        pair_ref[size:, :], eye - mm(matrix, pair_ref[size:, :])
+    )
+
+    @pl.when(high > 100.0 * low)
+    def _():
+        for _ in range(2):
+            inverse = pair_ref[size:, :]
+            pair_ref[size:, :] = inverse + mm(inverse, eye - mm(matrix, inverse))
+
+    return pair_ref[size:, :]
 
 
 def leaf_kernel(rank, levels, leaf_ref, bases_ref, targets_ref, solved_ref, *rest):
@@ -111,6 +133,26 @@
     return inverse + mm(inverse, eye - mm(matrix, inverse))
 
 
+def quick_solve(matrix, rhs, high):
+    size = matrix.shape[0]
+    eye = identity(size)
+    alpha = 2.0 / (1.0 + high)
+    residual = eye - alpha * matrix
+    inverse = alpha * (eye + residual)
+    residual = mm3(residual, residual)
+    for _ in range(2):
+        product = mm3(jnp.concatenate([residual, inverse], axis=0), residual)
+        inverse = inverse + product[size:]
+        residual = product[:size]
+    inverse = inverse + mm3(inverse, residual)
+    error = eye - mm(inverse, matrix)
+    found = mm(inverse, rhs)
+    worst = jnp.max(
+        jnp.sum(jnp.abs(error), axis=0, keepdims=True), axis=1, keepdims=True
+    )
+    return found + mm(error, found), worst
+
+
 def capacity_solve(front, weights, rank, doublings):
     width = front.shape[1] - rank
     eye = identity(rank)
@@ -121,25 +163,32 @@
     diag_col = jnp.sum(capacity * eye, axis=1, keepdims=True)
     root_row, root_col = lax.rsqrt(diag_row), lax.rsqrt(diag_col)
     scaled = capacity * root_row * root_col
+    sums = jnp.sum(jnp.abs(scaled), axis=0, keepdims=True)
+    high = jnp.broadcast_to(jnp.max(sums, axis=1, keepdims=True), (1, rank))
+    rhs = root_col * front[:, :width]
+    if not doublings:
+        found, worst = quick_solve(scaled, rhs, high)
+        return root_col * found, worst
     low = 0.99 * jnp.min(extra / diag_row, axis=1, keepdims=True)
-    sums = jnp.sum(jnp.abs(scaled), axis=0, keepdims=True)
-    high = jnp.max(sums, axis=1, keepdims=True)
     low = jnp.broadcast_to(low, (1, rank))
-    high = jnp.broadcast_to(high, (1, rank))
-    inverse = fixed_inverse(scaled, low, high, doublings)
-    return root_col * mm(inverse, root_col * front[:, :width])
+    return root_col * mm(fixed_inverse(scaled, low, high, doublings), rhs), None
 
 
 def tree_kernel(rank, levels, inner_bits, doublings, coupling_ref, solved_ref, *refs):
     pairs = [(k, j) for k in range(levels) for j in range(k, levels)]
     number = {pair: index for index, pair in enumerate(pairs)}
     first, refs = refs[:levels], refs[levels:]
-    out_ref, state_ref, refs = refs[0], refs[1], refs[2:]
+    if doublings:
+        (out_ref, state_ref), refs = refs[:2], refs[2:]
+    else:
+        (out_ref, flag_ref, state_ref), refs = refs[:3], refs[3:]
     landed = dict(zip(pairs, refs[: len(pairs)]))
     later = pairs[levels:]
     own = dict(zip(pairs[:levels], first))
     own.update(zip(later, refs[len(pairs) : len(pairs) + len(later)]))
-    send_sem, recv_sem = refs[-2:]
+    send_sem, recv_sem, load_sem = refs[-3:]
+    load = pltpu.make_async_copy(solved_ref, state_ref, load_sem)
+    load.start()
 
     group, inner = lax.axis_index("group"), lax.axis_index("inner")
 
@@ -171,12 +220,19 @@
 
     for j in range(levels):
         copy_of(0, j).start()
-    state_ref[...] = solved_ref[...]
+    bad = jnp.zeros((1, 1), jnp.float32)
     for k in range(levels):
         copy_of(k, k).wait_recv()
-        front = own[k, k][...] + landed[k, k][...]
+        front = own[k, k][:rank, :] + landed[k, k][:rank, :]
         wide = front.shape[1] - rank
-        coef = capacity_solve(front, coupling_ref[k : k + 1, :], rank, doublings)
+        coef, worst = capacity_solve(
+            front, coupling_ref[k : k + 1, :], rank, doublings
+        )
+        if not doublings:
+            if k > 0:
+                flags = jnp.maximum(own[k, k][rank:, :128], landed[k, k][rank:, :128])
+                bad = jnp.max(flags[:1, :], axis=1, keepdims=True)
+            bad = jnp.maximum(bad, worst)
         if k + 1 < levels:
             base = wide - rank * (levels - 1 - k)
             update = mm_t(front[:, base:wide], coef)
@@ -184,10 +240,16 @@
                 rows = rank * (levels - 1 - j)
                 columns = own[k, j].shape[1]
                 copy_of(k, j).wait_recv()
-                own[k + 1, j][...] = (own[k, j][...] + landed[k, j][...]) - update[
+                own[k + 1, j][:rank, :] = (own[k, j][...] + landed[k, j][...]) - update[
                     rows : rows + rank, :columns
                 ]
+                if j == k + 1 and not doublings:
+                    own[k + 1, j][rank:, :] = jnp.broadcast_to(
+                        bad, (FLAG_ROWS, columns)
+                    )
                 copy_of(k + 1, j).start()
+            if k == 0:
+                load.wait()
             state_ref[:, :wide] = state_ref[:, :wide] - mm(
                 state_ref[:, wide : wide + rank], coef
             )
@@ -195,8 +257,43 @@
             out_ref[...] = state_ref[:, :wide] - mm(
                 state_ref[:, wide : wide + rank], coef
             )
+    if not doublings:
+        flag_ref[...] = jnp.broadcast_to(bad, flag_ref.shape)
     for pair in pairs:
         copy_of(*pair).wait_send()
+
+
+def call_tree(coupling, solved, blocks, inner_bits, doublings):
+    levels, rank = coupling.shape
+    rows, width = solved.shape
+    right = width - rank * levels
+    f32 = jnp.float32
+    pairs = [(k, j) for k in range(levels) for j in range(k, levels)]
+    extra = 0 if doublings else FLAG_ROWS
+    landed = [
+        pltpu.VMEM((rank + (extra if j == k > 0 else 0), width - rank * j), f32)
+        for k, j in pairs
+    ]
+    result = [jax.ShapeDtypeStruct((rows, right), f32)]
+    if not doublings:
+        result.append(jax.ShapeDtypeStruct((FLAG_ROWS, 128), f32))
+    return pl.pallas_call(
+        functools.partial(tree_kernel, rank, levels, inner_bits, doublings),
+        out_shape=result,
+        in_specs=[VMEM, pl.BlockSpec(memory_space=pl.ANY)] + [VMEM] * levels,
+        out_specs=[VMEM] * len(result),
+        scratch_shapes=[pltpu.VMEM((rows, width), f32)]
+        + landed
+        + landed[levels:]
+        + [pltpu.SemaphoreType.DMA((len(pairs),))] * 2
+        + [pltpu.SemaphoreType.DMA],
+        compiler_params=pltpu.CompilerParams(
+            collective_id=1 if doublings else 0,
+            has_side_effects=True,
+            vmem_limit_bytes=60 * 2**20,
+        ),
+        name="careful" if doublings else "tree",
+    )(coupling, solved, *blocks)
 
 
 def per_device(leaf_blocks, bases, targets, coupling):
@@ -214,27 +311,17 @@
         in_specs=[VMEM] * 3,
         out_specs=[VMEM] * (1 + levels),
         scratch_shapes=[pltpu.VMEM((2 * size, size), f32)],
-        compiler_params=pltpu.CompilerParams(vmem_limit_bytes=32 * 2**20),
+        compiler_params=pltpu.CompilerParams(vmem_limit_bytes=60 * 2**20),
         name="leaf",
     )(leaf_blocks, bases.T, targets)
-    pairs = [(k, j) for k in range(levels) for j in range(k, levels)]
-    landed = [pltpu.VMEM((rank, widths[j]), f32) for _, j in pairs]
     worst = rank * (4.0 * rows * 2**levels / EIGEN_MIN + 1.0)
     doublings = math.ceil(math.log2(math.sqrt(worst) * 4.1))
-    return pl.pallas_call(
-        functools.partial(tree_kernel, rank, levels, inner_bits, doublings),
-        out_shape=jax.ShapeDtypeStruct((rows, right), f32),
-        in_specs=[VMEM] * (2 + levels),
-        out_specs=VMEM,
-        scratch_shapes=[pltpu.VMEM((rows, width), f32)]
-        + landed
-        + landed[levels:]
-        + [pltpu.SemaphoreType.DMA((len(pairs),))] * 2,
-        compiler_params=pltpu.CompilerParams(
-            collective_id=0, has_side_effects=True, vmem_limit_bytes=40 * 2**20
-        ),
-        name="tree",
-    )(coupling, solved, *blocks)
+    quick, flag = call_tree(coupling, solved, blocks, inner_bits, 0)
+    return lax.cond(
+        flag[0, 0] <= RESIDUAL_MAX,
+        lambda: quick,
+        lambda: call_tree(coupling, solved, blocks, inner_bits, doublings)[0],
+    )
 
 
 def solution(mesh):

time: 56.3 us -> 84.1 us (1.49)
  Pallas kernels: 51.9 us -> 80.5 us
  local copies, waits for them, and re-layouts: 4.17 us -> 2.53 us
    pallas_call x1 -> x2, Pallas kernels: 46.2 us -> 74.7 us  [call_tree(): pl.pallas_call(functools.partial(tree_kernel, rank, levels, inner_bits, d...]
    unnamed x9 -> x3, local copies, waits for them, and re-layouts: 4.17 us -> 1.34 us
    slice x0 -> x1, local copies, waits for them, and re-layouts: none -> 1.19 us  [per_device(): flag[0, 0] <= RESIDUAL_MAX]
where the time goes in v3:
time: 84.1 us; the launch traced here: 83.9 us
  Pallas kernels  80.5 us (96%)
  local copies, waits for them, and re-layouts  2.53 us (3%)
    pallas_call x2, Pallas kernels, call_tree(): pl.pallas_call(functools.partial(tree_kernel, rank, levels, inner_bits, d...  74.7 us
    pallas_call x1, Pallas kernels, per_device(): pl.pallas_call(functools.partial(leaf_kernel, rank, levels), out_shape=[j...  5.79 us

profile of v3, /device:TPU:0, one launch (start us, length us, event | category | flops | bytes accessed | tf_op | source)
XLA Modules:
  0.0 83.9 jit_solution(9973984393048102306)
XLA Ops:
  0.0 5.8 %leaf.1 = (f32[256,448]{1,0:T(8,128)S(1)}, f32[64,448]{1,0:T(8,128)S(1)}, f32[64,384]{1,0:T(8,128)S(1)}, f32[64,320]{1,0:T(8,128)S(1)}, f32[64,256]{1,0:T(8,128)S(1)}, /*index=5*/f32[64,192]{1,0:T(8,128)S(1)}) custom-call(f32[256,256]{1,0:T(8,128)} %leaf_ref.1, f32[320,256]{1,0:T(8,128)} %bitcast.2, f32[256,128]{1,0:T(8,128)} %targets_ref.1), custom_call_target="tpu_custom_call" | custom-call | tf_op jit(solution)/shard_map/leaf/pallas_call | solution.py:307
  5.8 0.0 copy-start
  5.8 0.7 copy-done
  6.5 34.6 %tree.1 = (f32[256,128]{1,0:T(8,128)S(1)}, f32[8,128]{1,0:T(8,128)}) custom-call(f32[5,64]{1,0:T(8,128)S(1)} %copy-done, f32[256,448]{1,0:T(8,128)S(1)} %get-tuple-element.38.solved_ref, f32[64,448]{1,0:T(8,128)S(1)} %get-tuple-element.39.refs_0_, f32[64,384]{1,0:T(8,128)S(1)} %get-tuple-element.40.refs_1_, f32[64,320]{1,0:T(8,128)S(1)} %get-tuple-element.41.refs_2_, ...), custom_call_target="tpu_custom_call" | custom-call | tf_op jit(solution)/shard_map/tree/pallas_call | solution.py:280
  41.1 1.2 %slice.3 = f32[1,1]{1,0:T(1,128)} slice(f32[8,128]{1,0:T(8,128)} %get-tuple-element.44), slice={[0:1], [0:1]} | slice | bytes 8 | tf_op jit(solution)/shard_map/slice | solution.py:321
  42.9 40.3 %conditional.1 = (f32[256,128]{1,0:T(8,128)S(1)}) conditional(s32[]{:T(128)} %bitcast.1, (f32[5,64]{1,0:T(8,128)S(1)}, f32[256,448]{1,0:T(8,128)S(1)}, f32[64,448]{1,0:T(8,128)S(1)}, f32[64,384]{1,0:T(8,128)S(1)}, f32[64,320]{1,0:T(8,128)S(1)}, /*index=5*/f32[64,256]{1,0:T(8,128)S(1)}, f32[64,192]{1,0:T(8,128)S(1)}) %tuple.17, ...), branch_computations={%region_0.0_spmd, %region_1.0_spmd} | conditional | bytes 8 | solution.py:320
  43.1 40.1 %careful.1 = f32[256,128]{1,0:T(8,128)S(1)} custom-call(f32[5,64]{1,0:T(8,128)S(1)} %get-tuple-element.23.coupling_ref, f32[256,448]{1,0:T(8,128)S(1)} %get-tuple-element.24.solved_ref, f32[64,448]{1,0:T(8,128)S(1)} %get-tuple-element.25.refs_0_, f32[64,384]{1,0:T(8,128)S(1)} %get-tuple-element.26.refs_1_, f32[64,320]{1,0:T(8,128)S(1)} %get-tuple-element.27.refs_2_, ...), custom_call_target="tpu_custom_call" | custom-call | tf_op jit(solution)/shard_map/cond/branch_0_fun/careful/pallas_call | solution.py:280
  83.3 0.7 copy.10
Async XLA Ops:
  5.8 0.7 copy-start

commit v4 on v3

--- a/solution.py
+++ b/solution.py
@@ -12,6 +12,7 @@
 LEAF_TOL = 3e-4
 RESIDUAL_MAX = 1e-3
 FLAG_ROWS = 8
+RELAX = 1.5
 VMEM = pl.BlockSpec(memory_space=pltpu.VMEM)
 
 
@@ -45,23 +46,13 @@
     )
 
 
-def mm_nt(first, second):
-    return lax.dot_general(
-        first,
-        second,
-        (((1,), (1,)), ((), ())),
-        precision=lax.Precision.HIGHEST,
-        preferred_element_type=jnp.float32,
-    )
-
-
 def identity(size):
     rows = lax.broadcasted_iota(jnp.int32, (size, size), 0)
     cols = lax.broadcasted_iota(jnp.int32, (size, size), 1)
     return jnp.where(rows == cols, 1.0, 0.0).astype(jnp.float32)
 
 
-def spd_inverse(matrix, low, high, pair_ref):
+def spd_solve(matrix, rhs, low, high, pair_ref):
     size = matrix.shape[0]
     eye = identity(size)
     alpha = 2.0 / (low + high)
@@ -81,9 +72,6 @@
         return square / (2.0 - square)
 
     lax.while_loop(cond, body, (high - low) / (high + low))
-    pair_ref[size:, :] = pair_ref[size:, :] + mm(
-        pair_ref[size:, :], eye - mm(matrix, pair_ref[size:, :])
-    )
 
     @pl.when(high > 100.0 * low)
     def _():
@@ -91,14 +79,15 @@
             inverse = pair_ref[size:, :]
             pair_ref[size:, :] = inverse + mm(inverse, eye - mm(matrix, inverse))
 
-    return pair_ref[size:, :]
+    both = mm(pair_ref[size:, :], jnp.concatenate([matrix, rhs], axis=1))
+    found = both[:, size:]
+    return found + mm3(eye - both[:, :size], found)
 
 
 def leaf_kernel(rank, levels, leaf_ref, bases_ref, targets_ref, solved_ref, *rest):
     blocks, pair_ref = rest[:levels], rest[levels]
     matrix = leaf_ref[...]
     high = jnp.max(jnp.sum(jnp.abs(matrix), axis=0, keepdims=True))
-    inverse = spd_inverse(matrix, EIGEN_MIN, jnp.maximum(high, 2 * EIGEN_MIN), pair_ref)
     flipped = jnp.concatenate(
         [
             bases_ref[rank * level : rank * (level + 1), :]
@@ -106,9 +95,9 @@
         ],
         axis=0,
     )
-    solved = jnp.concatenate(
-        [mm(inverse, targets_ref[...]), mm_nt(inverse, flipped)], axis=1
-    )
+    rhs = jnp.concatenate([targets_ref[...], flipped.T], axis=1)
+    high = jnp.maximum(high, 2 * EIGEN_MIN)
+    solved = spd_solve(matrix, rhs, EIGEN_MIN, high, pair_ref)
     solved_ref[...] = solved
     gram = mm(bases_ref[...], solved)
     for level in range(levels):
@@ -133,44 +122,41 @@
     return inverse + mm(inverse, eye - mm(matrix, inverse))
 
 
-def quick_solve(matrix, rhs, high):
+def quick_solve(matrix, rhs):
     size = matrix.shape[0]
     eye = identity(size)
-    alpha = 2.0 / (1.0 + high)
-    residual = eye - alpha * matrix
-    inverse = alpha * (eye + residual)
-    residual = mm3(residual, residual)
-    for _ in range(2):
+    residual = eye - matrix * (
+        RELAX / jnp.sum(jnp.abs(matrix), axis=0, keepdims=True)
+    )
+    inverse = eye * (RELAX / jnp.sum(jnp.abs(matrix), axis=0, keepdims=True))
+    for _ in range(3):
         product = mm3(jnp.concatenate([residual, inverse], axis=0), residual)
         inverse = inverse + product[size:]
         residual = product[:size]
     inverse = inverse + mm3(inverse, residual)
-    error = eye - mm(inverse, matrix)
-    found = mm(inverse, rhs)
-    worst = jnp.max(
-        jnp.sum(jnp.abs(error), axis=0, keepdims=True), axis=1, keepdims=True
-    )
-    return found + mm(error, found), worst
+    both = mm(inverse, jnp.concatenate([rhs, matrix], axis=1))
+    found = both[:, : rhs.shape[1]]
+    error = eye - both[:, rhs.shape[1] :]
+    worst = jnp.max(jnp.sum(jnp.abs(error), axis=0, keepdims=True))
+    return found + mm3(error, found), worst
 
 
 def capacity_solve(front, weights, rank, doublings):
     width = front.shape[1] - rank
     eye = identity(rank)
-    gram = front[:, width:]
     extra = 1.0 / weights
-    capacity = 0.5 * (gram + gram.T) + eye * extra
+    capacity = front[:, width:] + eye * extra
+    if not doublings:
+        return quick_solve(capacity, front[:, :width])
     diag_row = jnp.sum(capacity * eye, axis=0, keepdims=True)
     diag_col = jnp.sum(capacity * eye, axis=1, keepdims=True)
     root_row, root_col = lax.rsqrt(diag_row), lax.rsqrt(diag_col)
-    scaled = capacity * root_row * root_col
+    scaled = 0.5 * (capacity + capacity.T) * root_row * root_col
     sums = jnp.sum(jnp.abs(scaled), axis=0, keepdims=True)
     high = jnp.broadcast_to(jnp.max(sums, axis=1, keepdims=True), (1, rank))
-    rhs = root_col * front[:, :width]
-    if not doublings:
-        found, worst = quick_solve(scaled, rhs, high)
-        return root_col * found, worst
     low = 0.99 * jnp.min(extra / diag_row, axis=1, keepdims=True)
     low = jnp.broadcast_to(low, (1, rank))
+    rhs = root_col * front[:, :width]
     return root_col * mm(fixed_inverse(scaled, low, high, doublings), rhs), None
 
 
@@ -179,15 +165,17 @@
     number = {pair: index for index, pair in enumerate(pairs)}
     first, refs = refs[:levels], refs[levels:]
     if doublings:
-        (out_ref, state_ref), refs = refs[:2], refs[2:]
+        (rest_ref, coef_ref, state_ref), refs = refs[:3], refs[3:]
     else:
-        (out_ref, flag_ref, state_ref), refs = refs[:3], refs[3:]
+        (rest_ref, coef_ref, flag_ref, state_ref), refs = refs[:4], refs[4:]
     landed = dict(zip(pairs, refs[: len(pairs)]))
     later = pairs[levels:]
     own = dict(zip(pairs[:levels], first))
     own.update(zip(later, refs[len(pairs) : len(pairs) + len(later)]))
-    send_sem, recv_sem, load_sem = refs[-3:]
-    load = pltpu.make_async_copy(solved_ref, state_ref, load_sem)
+    weights_ref, send_sem, recv_sem, load_sem = refs[-4:]
+    load = pltpu.make_async_copy(solved_ref, state_ref, load_sem.at[0])
+    load_weights = pltpu.make_async_copy(coupling_ref, weights_ref, load_sem.at[1])
+    load_weights.start()
     load.start()
 
     group, inner = lax.axis_index("group"), lax.axis_index("inner")
@@ -220,18 +208,19 @@
 
     for j in range(levels):
         copy_of(0, j).start()
-    bad = jnp.zeros((1, 1), jnp.float32)
+    load_weights.wait()
+    bad = 0.0
     for k in range(levels):
         copy_of(k, k).wait_recv()
         front = own[k, k][:rank, :] + landed[k, k][:rank, :]
         wide = front.shape[1] - rank
         coef, worst = capacity_solve(
-            front, coupling_ref[k : k + 1, :], rank, doublings
+            front, weights_ref[k : k + 1, :], rank, doublings
         )
         if not doublings:
             if k > 0:
                 flags = jnp.maximum(own[k, k][rank:, :128], landed[k, k][rank:, :128])
-                bad = jnp.max(flags[:1, :], axis=1, keepdims=True)
+                bad = jnp.max(flags)
             bad = jnp.maximum(bad, worst)
         if k + 1 < levels:
             base = wide - rank * (levels - 1 - k)
@@ -244,21 +233,20 @@
                     rows : rows + rank, :columns
                 ]
                 if j == k + 1 and not doublings:
-                    own[k + 1, j][rank:, :] = jnp.broadcast_to(
-                        bad, (FLAG_ROWS, columns)
+                    own[k + 1, j][rank:, :] = jnp.full(
+                        (FLAG_ROWS, columns), bad, jnp.float32
                     )
                 copy_of(k + 1, j).start()
             if k == 0:
                 load.wait()
-            state_ref[:, :wide] = state_ref[:, :wide] - mm(
+            target = rest_ref if k + 2 == levels else state_ref
+            target[:, :wide] = state_ref[:, :wide] - mm(
                 state_ref[:, wide : wide + rank], coef
             )
         else:
-            out_ref[...] = state_ref[:, :wide] - mm(
-                state_ref[:, wide : wide + rank], coef
-            )
+            coef_ref[...] = coef
     if not doublings:
-        flag_ref[...] = jnp.broadcast_to(bad, flag_ref.shape)
+        flag_ref[0] = bad
     for pair in pairs:
         copy_of(*pair).wait_send()
 
@@ -274,19 +262,23 @@
         pltpu.VMEM((rank + (extra if j == k > 0 else 0), width - rank * j), f32)
         for k, j in pairs
     ]
-    result = [jax.ShapeDtypeStruct((rows, right), f32)]
+    result = [
+        jax.ShapeDtypeStruct((rows, right + rank), f32),
+        jax.ShapeDtypeStruct((rank, right), f32),
+    ]
     if not doublings:
-        result.append(jax.ShapeDtypeStruct((FLAG_ROWS, 128), f32))
+        result.append(jax.ShapeDtypeStruct((1,), f32))
     return pl.pallas_call(
         functools.partial(tree_kernel, rank, levels, inner_bits, doublings),
         out_shape=result,
-        in_specs=[VMEM, pl.BlockSpec(memory_space=pl.ANY)] + [VMEM] * levels,
-        out_specs=[VMEM] * len(result),
+        in_specs=[pl.BlockSpec(memory_space=pl.ANY)] * 2 + [VMEM] * levels,
+        out_specs=[VMEM] * 2 + [pl.BlockSpec(memory_space=pltpu.SMEM)] * (len(result) - 2),
         scratch_shapes=[pltpu.VMEM((rows, width), f32)]
         + landed
         + landed[levels:]
+        + [pltpu.VMEM((levels, rank), f32)]
         + [pltpu.SemaphoreType.DMA((len(pairs),))] * 2
-        + [pltpu.SemaphoreType.DMA],
+        + [pltpu.SemaphoreType.DMA((2,))],
         compiler_params=pltpu.CompilerParams(
             collective_id=1 if doublings else 0,
             has_side_effects=True,
@@ -294,6 +286,21 @@
         ),
         name="careful" if doublings else "tree",
     )(coupling, solved, *blocks)
+
+
+def last_kernel(rest_ref, coef_ref, out_ref):
+    width = out_ref.shape[1]
+    out_ref[...] = rest_ref[:, :width] - mm(rest_ref[:, width:], coef_ref[...])
+
+
+def last_update(rest, coef):
+    return pl.pallas_call(
+        last_kernel,
+        out_shape=jax.ShapeDtypeStruct((rest.shape[0], coef.shape[1]), jnp.float32),
+        in_specs=[VMEM] * 2,
+        out_specs=VMEM,
+        name="last",
+    )(rest, coef)
 
 
 def per_device(leaf_blocks, bases, targets, coupling):
@@ -316,11 +323,13 @@
     )(leaf_blocks, bases.T, targets)
     worst = rank * (4.0 * rows * 2**levels / EIGEN_MIN + 1.0)
     doublings = math.ceil(math.log2(math.sqrt(worst) * 4.1))
-    quick, flag = call_tree(coupling, solved, blocks, inner_bits, 0)
+    rest, coef, flag = call_tree(coupling, solved, blocks, inner_bits, 0)
+
+    def careful():
+        return last_update(*call_tree(coupling, solved, blocks, inner_bits, doublings))
+
     return lax.cond(
-        flag[0, 0] <= RESIDUAL_MAX,
-        lambda: quick,
-        lambda: call_tree(coupling, solved, blocks, inner_bits, doublings)[0],
+        flag[0] <= RESIDUAL_MAX, lambda: last_update(rest, coef), careful
     )
 
 

time: 84.1 us -> 82.1 us (0.976)
  local copies, waits for them, and re-layouts: 2.53 us -> 1.33 us
    pallas_call x2, Pallas kernels: 74.7 us -> 73.2 us  [call_tree(): pl.pallas_call(functools.partial(tree_kernel, rank, levels, inner_bits, d...]
    pallas_call x0 -> x1, Pallas kernels: none -> 1.2 us  [last_update(): pl.pallas_call(last_kernel, out_shape=jax.ShapeDtypeStruct((rest.shape[0]...]
    slice x1 -> x0, local copies, waits for them, and re-layouts: 1.19 us -> none  [per_device(): flag[0, 0] <= RESIDUAL_MAX]
where the time goes in v4:
time: 82.1 us; the launch traced here: 81.9 us
  Pallas kernels  79.8 us (97%)
  local copies, waits for them, and re-layouts  1.33 us (2%)
    pallas_call x2, Pallas kernels, call_tree(): pl.pallas_call(functools.partial(tree_kernel, rank, levels, inner_bits, d...  73.2 us
    pallas_call x1, Pallas kernels, per_device(): pl.pallas_call(functools.partial(leaf_kernel, rank, levels), out_shape=[j...  5.42 us

profile of v4, /device:TPU:0, one launch (start us, length us, event | category | flops | bytes accessed | tf_op | source)
XLA Modules:
  0.0 81.9 jit_solution(2668859254080618171)
XLA Ops:
  0.0 5.4 %leaf.1 = (f32[256,448]{1,0:T(8,128)S(1)}, f32[64,448]{1,0:T(8,128)S(1)}, f32[64,384]{1,0:T(8,128)S(1)}, f32[64,320]{1,0:T(8,128)S(1)}, f32[64,256]{1,0:T(8,128)S(1)}, /*index=5*/f32[64,192]{1,0:T(8,128)S(1)}) custom-call(f32[256,256]{1,0:T(8,128)} %leaf_ref.1, f32[320,256]{1,0:T(8,128)} %bitcast.2, f32[256,128]{1,0:T(8,128)} %targets_ref.1), custom_call_target="tpu_custom_call" | custom-call | tf_op jit(solution)/shard_map/leaf/pallas_call | solution.py:314
  5.4 0.0 copy-start.1
  5.4 0.7 copy-done.1
  6.1 34.1 %tree.1 = (f32[256,192]{1,0:T(8,128)S(1)}, f32[64,128]{1,0:T(8,128)S(1)}, f32[1]{0:T(128)}) custom-call(f32[5,64]{1,0:T(8,128)S(1)} %copy-done.1, f32[256,448]{1,0:T(8,128)S(1)} %get-tuple-element.46.solved_ref, f32[64,448]{1,0:T(8,128)S(1)} %get-tuple-element.47.refs_0_, f32[64,384]{1,0:T(8,128)S(1)} %get-tuple-element.48.refs_1_, ...), custom_call_target="tpu_custom_call" | custom-call | tf_op jit(solution)/shard_map/tree/pallas_call | solution.py:271
  40.8 40.5 %conditional.1 = (f32[256,128]{1,0:T(8,128)S(1)}) conditional(s32[]{:T(128)} %bitcast.1, (f32[5,64]{1,0:T(8,128)S(1)}, f32[256,448]{1,0:T(8,128)S(1)}, f32[64,448]{1,0:T(8,128)S(1)}, f32[64,384]{1,0:T(8,128)S(1)}, f32[64,320]{1,0:T(8,128)S(1)}, /*index=5*/f32[64,256]{1,0:T(8,128)S(1)}, f32[64,192]{1,0:T(8,128)S(1)}) %tuple.18, ...), branch_computations={%region_0.0_spmd, %region_1.0_spmd} | conditional | bytes 8 | solution.py:331
  41.0 39.1 %careful.1 = (f32[256,192]{1,0:T(8,128)}, f32[64,128]{1,0:T(8,128)}) custom-call(f32[5,64]{1,0:T(8,128)S(1)} %get-tuple-element.26.coupling_ref, f32[256,448]{1,0:T(8,128)S(1)} %get-tuple-element.27.solved_ref, f32[64,448]{1,0:T(8,128)S(1)} %get-tuple-element.28.refs_0_, f32[64,384]{1,0:T(8,128)S(1)} %get-tuple-element.29.refs_1_, ...), custom_call_target="tpu_custom_call" | custom-call | tf_op jit(solution)/shard_map/cond/branch_0_fun/careful/pallas_call | solution.py:271
  80.0 1.2 %last.2 = f32[256,128]{1,0:T(8,128)S(1)} custom-call(f32[256,192]{1,0:T(8,128)} %get-tuple-element.33.rest_ref, f32[64,128]{1,0:T(8,128)} %get-tuple-element.34.coef_ref), custom_call_target="tpu_custom_call" | custom-call | tf_op jit(solution)/shard_map/cond/branch_0_fun/last/pallas_call | solution.py:297
  81.3 0.0 copy-start
  81.3 0.6 copy-done
Async XLA Ops:
  5.4 0.7 copy-start.1
  81.3 0.7 copy-start

commit v5 on v4

--- a/solution.py
+++ b/solution.py
@@ -84,8 +84,10 @@
     return found + mm3(eye - both[:, :size], found)
 
 
-def leaf_kernel(rank, levels, leaf_ref, bases_ref, targets_ref, solved_ref, *rest):
+def leaf_kernel(rank, levels, leaf_ref, bases_ref, targets_ref, coupling_ref, *rest):
+    solved_ref, extra_ref, rest = rest[0], rest[1], rest[2:]
     blocks, pair_ref = rest[:levels], rest[levels]
+    extra_ref[...] = 1.0 / coupling_ref[...]
     matrix = leaf_ref[...]
     high = jnp.max(jnp.sum(jnp.abs(matrix), axis=0, keepdims=True))
     flipped = jnp.concatenate(
@@ -122,7 +124,7 @@
     return inverse + mm(inverse, eye - mm(matrix, inverse))
 
 
-def quick_solve(matrix, rhs):
+def quick_solve(matrix, rhs, between):
     size = matrix.shape[0]
     eye = identity(size)
     residual = eye - matrix * (
@@ -134,20 +136,21 @@
         inverse = inverse + product[size:]
         residual = product[:size]
     inverse = inverse + mm3(inverse, residual)
+    between()
     both = mm(inverse, jnp.concatenate([rhs, matrix], axis=1))
     found = both[:, : rhs.shape[1]]
     error = eye - both[:, rhs.shape[1] :]
-    worst = jnp.max(jnp.sum(jnp.abs(error), axis=0, keepdims=True))
+    worst = jnp.sum(jnp.abs(error), axis=0, keepdims=True)
     return found + mm3(error, found), worst
 
 
-def capacity_solve(front, weights, rank, doublings):
+def capacity_solve(front, extra, rank, doublings, between):
     width = front.shape[1] - rank
     eye = identity(rank)
-    extra = 1.0 / weights
     capacity = front[:, width:] + eye * extra
     if not doublings:
-        return quick_solve(capacity, front[:, :width])
+        return quick_solve(capacity, front[:, :width], between)
+    between()
     diag_row = jnp.sum(capacity * eye, axis=0, keepdims=True)
     diag_col = jnp.sum(capacity * eye, axis=1, keepdims=True)
     root_row, root_col = lax.rsqrt(diag_row), lax.rsqrt(diag_col)
@@ -160,7 +163,7 @@
     return root_col * mm(fixed_inverse(scaled, low, high, doublings), rhs), None
 
 
-def tree_kernel(rank, levels, inner_bits, doublings, coupling_ref, solved_ref, *refs):
+def tree_kernel(rank, levels, inner_bits, doublings, extra_ref, solved_ref, *refs):
     pairs = [(k, j) for k in range(levels) for j in range(k, levels)]
     number = {pair: index for index, pair in enumerate(pairs)}
     first, refs = refs[:levels], refs[levels:]
@@ -172,11 +175,12 @@
     later = pairs[levels:]
     own = dict(zip(pairs[:levels], first))
     own.update(zip(later, refs[len(pairs) : len(pairs) + len(later)]))
-    weights_ref, send_sem, recv_sem, load_sem = refs[-4:]
-    load = pltpu.make_async_copy(solved_ref, state_ref, load_sem.at[0])
-    load_weights = pltpu.make_async_copy(coupling_ref, weights_ref, load_sem.at[1])
-    load_weights.start()
+    send_sem, recv_sem, load_sem = refs[-3:]
+    load = pltpu.make_async_copy(solved_ref, state_ref, load_sem)
     load.start()
+    if not doublings:
+        for k in range(1, levels):
+            own[k, k][rank:, :] = jnp.zeros((FLAG_ROWS, own[k, k].shape[1]), jnp.float32)
 
     group, inner = lax.axis_index("group"), lax.axis_index("inner")
 
@@ -206,60 +210,75 @@
         )
     pl.semaphore_wait(barrier, levels)
 
-    for j in range(levels):
-        copy_of(0, j).start()
-    load_weights.wait()
-    bad = 0.0
+    sent = []
+
+    def send(k, j):
+        if (k, j - 1) in pairs:
+            copy_of(k, j - 1).wait_send()
+            sent.append((k, j - 1))
+        copy_of(k, j).start()
+
+    def send_first(j):
+        if j < levels:
+            send(0, j)
+
+    send_first(0)
+    send_first(1)
+    bad = jnp.zeros((1, rank), jnp.float32)
     for k in range(levels):
         copy_of(k, k).wait_recv()
         front = own[k, k][:rank, :] + landed[k, k][:rank, :]
         wide = front.shape[1] - rank
+        base = wide - rank * (levels - 1 - k)
+        turned = front[:, base:wide].T if k + 1 < levels else None
         coef, worst = capacity_solve(
-            front, weights_ref[k : k + 1, :], rank, doublings
+            front,
+            extra_ref[k : k + 1, :],
+            rank,
+            doublings,
+            lambda: send_first(2) if k == 0 else None,
         )
         if not doublings:
             if k > 0:
-                flags = jnp.maximum(own[k, k][rank:, :128], landed[k, k][rank:, :128])
-                bad = jnp.max(flags)
+                flags = jnp.maximum(own[k, k][rank:, :rank], landed[k, k][rank:, :rank])
+                bad = jnp.maximum(bad, flags[:1, :])
             bad = jnp.maximum(bad, worst)
-        if k + 1 < levels:
-            base = wide - rank * (levels - 1 - k)
-            update = mm_t(front[:, base:wide], coef)
-            for j in range(k + 1, levels):
-                rows = rank * (levels - 1 - j)
-                columns = own[k, j].shape[1]
-                copy_of(k, j).wait_recv()
-                own[k + 1, j][:rank, :] = (own[k, j][...] + landed[k, j][...]) - update[
-                    rows : rows + rank, :columns
-                ]
-                if j == k + 1 and not doublings:
-                    own[k + 1, j][rank:, :] = jnp.full(
-                        (FLAG_ROWS, columns), bad, jnp.float32
-                    )
-                copy_of(k + 1, j).start()
+        if k + 1 == levels:
+            coef_ref[...] = coef
+        for j in range(k + 1, levels):
+            rows = rank * (levels - 1 - j)
+            columns = own[k, j].shape[1]
+            update = mm(turned[rows : rows + rank, :], coef[:, :columns])
+            copy_of(k, j).wait_recv()
+            own[k + 1, j][:rank, :] = own[k, j][...] + landed[k, j][...] - update
+            if j == k + 1 and not doublings:
+                own[k + 1, j][rank:, :rank] = jnp.broadcast_to(bad, (FLAG_ROWS, rank))
+            send(k + 1, j)
             if k == 0:
-                load.wait()
-            target = rest_ref if k + 2 == levels else state_ref
-            target[:, :wide] = state_ref[:, :wide] - mm(
-                state_ref[:, wide : wide + rank], coef
-            )
-        else:
-            coef_ref[...] = coef
+                send_first(j + 2)
+            if j == k + 1:
+                if k == 0:
+                    load.wait()
+                target = rest_ref if k + 2 == levels else state_ref
+                target[:, :wide] = state_ref[:, :wide] - mm(
+                    state_ref[:, wide : wide + rank], coef
+                )
     if not doublings:
-        flag_ref[0] = bad
+        flag_ref[0] = jnp.max(bad)
     for pair in pairs:
-        copy_of(*pair).wait_send()
-
-
-def call_tree(coupling, solved, blocks, inner_bits, doublings):
-    levels, rank = coupling.shape
+        if pair not in sent:
+            copy_of(*pair).wait_send()
+
+
+def call_tree(extra, solved, blocks, inner_bits, doublings):
+    levels, rank = extra.shape
     rows, width = solved.shape
     right = width - rank * levels
     f32 = jnp.float32
     pairs = [(k, j) for k in range(levels) for j in range(k, levels)]
-    extra = 0 if doublings else FLAG_ROWS
+    flag_rows = 0 if doublings else FLAG_ROWS
     landed = [
-        pltpu.VMEM((rank + (extra if j == k > 0 else 0), width - rank * j), f32)
+        pltpu.VMEM((rank + (flag_rows if j == k > 0 else 0), width - rank * j), f32)
         for k, j in pairs
     ]
     result = [
@@ -271,21 +290,20 @@
     return pl.pallas_call(
         functools.partial(tree_kernel, rank, levels, inner_bits, doublings),
         out_shape=result,
-        in_specs=[pl.BlockSpec(memory_space=pl.ANY)] * 2 + [VMEM] * levels,
+        in_specs=[VMEM, pl.BlockSpec(memory_space=pl.ANY)] + [VMEM] * levels,
         out_specs=[VMEM] * 2 + [pl.BlockSpec(memory_space=pltpu.SMEM)] * (len(result) - 2),
         scratch_shapes=[pltpu.VMEM((rows, width), f32)]
         + landed
         + landed[levels:]
-        + [pltpu.VMEM((levels, rank), f32)]
         + [pltpu.SemaphoreType.DMA((len(pairs),))] * 2
-        + [pltpu.SemaphoreType.DMA((2,))],
+        + [pltpu.SemaphoreType.DMA],
         compiler_params=pltpu.CompilerParams(
             collective_id=1 if doublings else 0,
             has_side_effects=True,
             vmem_limit_bytes=60 * 2**20,
         ),
         name="careful" if doublings else "tree",
-    )(coupling, solved, *blocks)
+    )(extra, solved, *blocks)
 
 
 def last_kernel(rest_ref, coef_ref, out_ref):
@@ -299,6 +317,7 @@
         out_shape=jax.ShapeDtypeStruct((rest.shape[0], coef.shape[1]), jnp.float32),
         in_specs=[VMEM] * 2,
         out_specs=VMEM,
+        compiler_params=pltpu.CompilerParams(vmem_limit_bytes=60 * 2**20),
         name="last",
     )(rest, coef)
 
@@ -311,22 +330,25 @@
     inner_bits = lax.axis_size("inner").bit_length() - 1
     f32 = jnp.float32
     widths = [width - rank * level for level in range(levels)]
-    solved, *blocks = pl.pallas_call(
+    solved, extra, *blocks = pl.pallas_call(
         functools.partial(leaf_kernel, rank, levels),
-        out_shape=[jax.ShapeDtypeStruct((rows, width), f32)]
+        out_shape=[
+            jax.ShapeDtypeStruct((rows, width), f32),
+            jax.ShapeDtypeStruct((levels, rank), f32),
+        ]
         + [jax.ShapeDtypeStruct((rank, wide), f32) for wide in widths],
-        in_specs=[VMEM] * 3,
-        out_specs=[VMEM] * (1 + levels),
+        in_specs=[VMEM] * 4,
+        out_specs=[VMEM] * (2 + levels),
         scratch_shapes=[pltpu.VMEM((2 * size, size), f32)],
         compiler_params=pltpu.CompilerParams(vmem_limit_bytes=60 * 2**20),
         name="leaf",
-    )(leaf_blocks, bases.T, targets)
+    )(leaf_blocks, bases.T, targets, coupling)
     worst = rank * (4.0 * rows * 2**levels / EIGEN_MIN + 1.0)
     doublings = math.ceil(math.log2(math.sqrt(worst) * 4.1))
-    rest, coef, flag = call_tree(coupling, solved, blocks, inner_bits, 0)
+    rest, coef, flag = call_tree(extra, solved, blocks, inner_bits, 0)
 
     def careful():
-        return last_update(*call_tree(coupling, solved, blocks, inner_bits, doublings))
+        return last_update(*call_tree(extra, solved, blocks, inner_bits, doublings))
 
     return lax.cond(
         flag[0] <= RESIDUAL_MAX, lambda: last_update(rest, coef), careful

time: 82.1 us -> 90.6 us (1.10)
  Pallas kernels: 79.8 us -> 88.9 us
    pallas_call x2, Pallas kernels: 73.2 us -> 82.2 us  [call_tree(): pl.pallas_call(functools.partial(tree_kernel, rank, levels, inner_bits, d...]
where the time goes in v5:
time: 90.6 us; the launch traced here: 90.4 us
  Pallas kernels  88.9 us (98%)
    pallas_call x2, Pallas kernels, call_tree(): pl.pallas_call(functools.partial(tree_kernel, rank, levels, inner_bits, d...  82.2 us
    pallas_call x1, Pallas kernels, per_device(): pl.pallas_call(functools.partial(leaf_kernel, rank, levels), out_shape=[j...  5.42 us

profile of v5, /device:TPU:0, one launch (start us, length us, event | category | flops | bytes accessed | tf_op | source)
XLA Modules:
  0.0 90.4 jit_solution(3452872034851406592)
XLA Ops:
  0.0 5.4 %leaf.1 = (f32[256,448]{1,0:T(8,128)S(1)}, f32[5,64]{1,0:T(8,128)S(1)}, f32[64,448]{1,0:T(8,128)S(1)}, f32[64,384]{1,0:T(8,128)S(1)}, f32[64,320]{1,0:T(8,128)S(...) custom-call(f32[256,256]{1,0:T(8,128)} %leaf_ref.1, f32[320,256]{1,0:T(8,128)} %bitcast.2, f32[256,128]{1,0:T(8,128)} %targets_ref.1, ...), custom_call_target="tpu_custom_call" | custom-call | tf_op jit(solution)/shard_map/leaf/pallas_call | solution.py:333
  5.4 37.7 %tree.1 = (f32[256,192]{1,0:T(8,128)S(1)}, f32[64,128]{1,0:T(8,128)S(1)}, f32[1]{0:T(128)}) custom-call(f32[5,64]{1,0:T(8,128)S(1)} %get-tuple-element.47.extra_ref, f32[256,448]{1,0:T(8,128)S(1)} %get-tuple-element.48.solved_ref, f32[64,448]{1,0:T(8,128)S(1)} %get-tuple-element.49.refs_0_, f32[64,384]{1,0:T(8,128)S(1)} %get-tuple-element.50.refs_1_, ...), custom_call_target="tpu_custom_call" | custom-call | tf_op jit(solution)/shard_map/tree/pallas_call | solution.py:290
  43.8 45.9 %conditional.1 = (f32[256,128]{1,0:T(8,128)S(1)}) conditional(s32[]{:T(128)} %bitcast.1, (f32[5,64]{1,0:T(8,128)S(1)}, f32[256,448]{1,0:T(8,128)S(1)}, f32[64,448]{1,0:T(8,128)S(1)}, f32[64,384]{1,0:T(8,128)S(1)}, f32[64,320]{1,0:T(8,128)S(1)}, /*index=5*/f32[64,256]{1,0:T(8,128)S(1)}, f32[64,192]{1,0:T(8,128)S(1)}) %tuple.11, ...), branch_computations={%region_0.0_spmd, %region_1.0_spmd} | conditional | bytes 8 | solution.py:353
  44.0 44.5 %careful.1 = (f32[256,192]{1,0:T(8,128)}, f32[64,128]{1,0:T(8,128)}) custom-call(f32[5,64]{1,0:T(8,128)S(1)} %get-tuple-element.26.extra_ref, f32[256,448]{1,0:T(8,128)S(1)} %get-tuple-element.27.solved_ref, f32[64,448]{1,0:T(8,128)S(1)} %get-tuple-element.28.refs_0_, f32[64,384]{1,0:T(8,128)S(1)} %get-tuple-element.29.refs_1_, ...), custom_call_target="tpu_custom_call" | custom-call | tf_op jit(solution)/shard_map/cond/branch_0_fun/careful/pallas_call | solution.py:290
  88.6 1.2 %last.2 = f32[256,128]{1,0:T(8,128)S(1)} custom-call(f32[256,192]{1,0:T(8,128)} %get-tuple-element.33.rest_ref, f32[64,128]{1,0:T(8,128)} %get-tuple-element.34.coef_ref), custom_call_target="tpu_custom_call" | custom-call | tf_op jit(solution)/shard_map/cond/branch_0_fun/last/pallas_call | solution.py:315
  89.8 0.0 copy-start
  89.8 0.6 copy-done
Async XLA Ops:
  89.8 0.7 copy-start

commit v6 on v5

--- a/solution.py
+++ b/solution.py
@@ -13,6 +13,7 @@
 RESIDUAL_MAX = 1e-3
 FLAG_ROWS = 8
 RELAX = 1.5
+LANES = 128
 VMEM = pl.BlockSpec(memory_space=pltpu.VMEM)
 
 
@@ -44,6 +45,30 @@
         precision=lax.Precision.HIGHEST,
         preferred_element_type=jnp.float32,
     )
+
+
+def packed_rows(rank, width):
+    return rank * (width // LANES) + (rank // 2 if width % LANES else 0)
+
+
+def pack(value):
+    rank, width = value.shape
+    full = width // LANES
+    tiles = [value[:, LANES * t : LANES * (t + 1)] for t in range(full)]
+    if width % LANES:
+        tail = value[:, LANES * full :]
+        tiles.append(jnp.concatenate([tail[: rank // 2], tail[rank // 2 :]], axis=1))
+    return jnp.concatenate(tiles, axis=0)
+
+
+def unpack(value, rank, width):
+    full = width // LANES
+    tiles = [value[rank * t : rank * (t + 1), :] for t in range(full)]
+    if width % LANES:
+        tail = value[rank * full :, :]
+        half = LANES // 2
+        tiles.append(jnp.concatenate([tail[:, :half], tail[:, half:]], axis=0))
+    return jnp.concatenate(tiles, axis=1)
 
 
 def identity(size):
@@ -104,7 +129,7 @@
     gram = mm(bases_ref[...], solved)
     for level in range(levels):
         width = solved.shape[1] - rank * level
-        blocks[level][...] = gram[rank * level : rank * (level + 1), :width]
+        blocks[level][...] = pack(gram[rank * level : rank * (level + 1), :width])
 
 
 def fixed_inverse(matrix, low, high, doublings):
@@ -124,19 +149,18 @@
     return inverse + mm(inverse, eye - mm(matrix, inverse))
 
 
-def quick_solve(matrix, rhs, between):
+def quick_solve(matrix, rhs, squarings):
     size = matrix.shape[0]
     eye = identity(size)
     residual = eye - matrix * (
         RELAX / jnp.sum(jnp.abs(matrix), axis=0, keepdims=True)
     )
     inverse = eye * (RELAX / jnp.sum(jnp.abs(matrix), axis=0, keepdims=True))
-    for _ in range(3):
+    for _ in range(squarings - 1):
         product = mm3(jnp.concatenate([residual, inverse], axis=0), residual)
         inverse = inverse + product[size:]
         residual = product[:size]
     inverse = inverse + mm3(inverse, residual)
-    between()
     both = mm(inverse, jnp.concatenate([rhs, matrix], axis=1))
     found = both[:, : rhs.shape[1]]
     error = eye - both[:, rhs.shape[1] :]
@@ -144,13 +168,12 @@
     return found + mm3(error, found), worst
 
 
-def capacity_solve(front, extra, rank, doublings, between):
+def capacity_solve(front, extra, rank, doublings, squarings):
     width = front.shape[1] - rank
     eye = identity(rank)
     capacity = front[:, width:] + eye * extra
     if not doublings:
-        return quick_solve(capacity, front[:, :width], between)
-    between()
+        return quick_solve(capacity, front[:, :width], squarings)
     diag_row = jnp.sum(capacity * eye, axis=0, keepdims=True)
     diag_col = jnp.sum(capacity * eye, axis=1, keepdims=True)
     root_row, root_col = lax.rsqrt(diag_row), lax.rsqrt(diag_col)
@@ -178,9 +201,11 @@
     send_sem, recv_sem, load_sem = refs[-3:]
     load = pltpu.make_async_copy(solved_ref, state_ref, load_sem)
     load.start()
+    widths = [solved_ref.shape[1] - rank * j for j in range(levels)]
+    heights = [packed_rows(rank, wide) for wide in widths]
     if not doublings:
         for k in range(1, levels):
-            own[k, k][rank:, :] = jnp.zeros((FLAG_ROWS, own[k, k].shape[1]), jnp.float32)
+            own[k, k][heights[k] :, :] = jnp.zeros((FLAG_ROWS, LANES), jnp.float32)
 
     group, inner = lax.axis_index("group"), lax.axis_index("inner")
 
@@ -210,24 +235,14 @@
         )
     pl.semaphore_wait(barrier, levels)
 
-    sent = []
-
-    def send(k, j):
-        if (k, j - 1) in pairs:
-            copy_of(k, j - 1).wait_send()
-            sent.append((k, j - 1))
-        copy_of(k, j).start()
-
-    def send_first(j):
-        if j < levels:
-            send(0, j)
-
-    send_first(0)
-    send_first(1)
+    for j in range(levels):
+        copy_of(0, j).start()
     bad = jnp.zeros((1, rank), jnp.float32)
     for k in range(levels):
         copy_of(k, k).wait_recv()
-        front = own[k, k][:rank, :] + landed[k, k][:rank, :]
+        height = heights[k]
+        front = own[k, k][:height, :] + landed[k, k][:height, :]
+        front = unpack(front, rank, widths[k])
         wide = front.shape[1] - rank
         base = wide - rank * (levels - 1 - k)
         turned = front[:, base:wide].T if k + 1 < levels else None
@@ -236,26 +251,26 @@
             extra_ref[k : k + 1, :],
             rank,
             doublings,
-            lambda: send_first(2) if k == 0 else None,
+            5 if k == 0 else 4,
         )
         if not doublings:
             if k > 0:
-                flags = jnp.maximum(own[k, k][rank:, :rank], landed[k, k][rank:, :rank])
-                bad = jnp.maximum(bad, flags[:1, :])
+                flags = jnp.maximum(own[k, k][height:, :], landed[k, k][height:, :])
+                bad = jnp.maximum(bad, flags[:1, :rank])
             bad = jnp.maximum(bad, worst)
         if k + 1 == levels:
             coef_ref[...] = coef
         for j in range(k + 1, levels):
             rows = rank * (levels - 1 - j)
-            columns = own[k, j].shape[1]
-            update = mm(turned[rows : rows + rank, :], coef[:, :columns])
+            update = pack(mm(turned[rows : rows + rank, :], coef[:, : widths[j]]))
             copy_of(k, j).wait_recv()
-            own[k + 1, j][:rank, :] = own[k, j][...] + landed[k, j][...] - update
+            total = own[k, j][...] + landed[k, j][...] - update
+            own[k + 1, j][: heights[j], :] = total
             if j == k + 1 and not doublings:
-                own[k + 1, j][rank:, :rank] = jnp.broadcast_to(bad, (FLAG_ROWS, rank))
-            send(k + 1, j)
-            if k == 0:
-                send_first(j + 2)
+                own[k + 1, j][heights[j] :, :rank] = jnp.broadcast_to(
+                    bad, (FLAG_ROWS, rank)
+                )
+            copy_of(k + 1, j).start()
             if j == k + 1:
                 if k == 0:
                     load.wait()
@@ -266,8 +281,7 @@
     if not doublings:
         flag_ref[0] = jnp.max(bad)
     for pair in pairs:
-        if pair not in sent:
-            copy_of(*pair).wait_send()
+        copy_of(*pair).wait_send()
 
 
 def call_tree(extra, solved, blocks, inner_bits, doublings):
@@ -278,7 +292,13 @@
     pairs = [(k, j) for k in range(levels) for j in range(k, levels)]
     flag_rows = 0 if doublings else FLAG_ROWS
     landed = [
-        pltpu.VMEM((rank + (flag_rows if j == k > 0 else 0), width - rank * j), f32)
+        pltpu.VMEM(
+            (
+                packed_rows(rank, width - rank * j) + (flag_rows if j == k > 0 else 0),
+                LANES,
+            ),
+            f32,
+        )
         for k, j in pairs
     ]
     result = [
@@ -336,7 +356,7 @@
             jax.ShapeDtypeStruct((rows, width), f32),
             jax.ShapeDtypeStruct((levels, rank), f32),
         ]
-        + [jax.ShapeDtypeStruct((rank, wide), f32) for wide in widths],
+        + [jax.ShapeDtypeStruct((packed_rows(rank, wide), LANES), f32) for wide in widths],
         in_specs=[VMEM] * 4,
         out_specs=[VMEM] * (2 + levels),
         scratch_shapes=[pltpu.VMEM((2 * size, size), f32)],

time: 90.6 us -> 79.9 us (0.88)
  Pallas kernels: 88.9 us -> 78.1 us
    pallas_call x2, Pallas kernels: 82.2 us -> 71.5 us  [call_tree(): pl.pallas_call(functools.partial(tree_kernel, rank, levels, inner_bits, d...]
where the time goes in v6:
time: 79.9 us; the launch traced here: 79.7 us
  Pallas kernels  78.1 us (98%)
    pallas_call x2, Pallas kernels, call_tree(): pl.pallas_call(functools.partial(tree_kernel, rank, levels, inner_bits, d...  71.5 us
    pallas_call x1, Pallas kernels, per_device(): pl.pallas_call(functools.partial(leaf_kernel, rank, levels), out_shape=[j...  5.47 us

profile of v6, /device:TPU:0, one launch (start us, length us, event | category | flops | bytes accessed | tf_op | source)
XLA Modules:
  0.0 79.7 jit_solution(12035589358749158108)
XLA Ops:
  0.0 5.5 %leaf.1 = (f32[256,448]{1,0:T(8,128)S(1)}, f32[5,64]{1,0:T(8,128)S(1)}, f32[224,128]{1,0:T(8,128)S(1)}, f32[192,128]{1,0:T(8,128)S(1)}, f32[160,128]{1,0:T(8,128...) custom-call(f32[256,256]{1,0:T(8,128)} %leaf_ref.1, f32[320,256]{1,0:T(8,128)} %bitcast.2, f32[256,128]{1,0:T(8,128)} %targets_ref.1, ...), custom_call_target="tpu_custom_call" | custom-call | tf_op jit(solution)/shard_map/leaf/pallas_call | solution.py:353
  5.5 32.4 %tree.1 = (f32[256,192]{1,0:T(8,128)S(1)}, f32[64,128]{1,0:T(8,128)S(1)}, f32[1]{0:T(128)}) custom-call(f32[5,64]{1,0:T(8,128)S(1)} %get-tuple-element.47.extra_ref, f32[256,448]{1,0:T(8,128)S(1)} %get-tuple-element.48.solved_ref, f32[224,128]{1,0:T(8,128)S(1)} %get-tuple-element.49.refs_0_, f32[192,128]{1,0:T(8,128)S(1)} %get-tuple-element.50.refs_1_, ...), custom_call_target="tpu_custom_call" | custom-call | tf_op jit(solution)/shard_map/tree/pallas_call | solution.py:310
  38.6 40.4 %conditional.1 = (f32[256,128]{1,0:T(8,128)S(1)}) conditional(s32[]{:T(128)} %bitcast.1, (f32[5,64]{1,0:T(8,128)S(1)}, f32[256,448]{1,0:T(8,128)S(1)}, f32[224,128]{1,0:T(8,128)S(1)}, f32[192,128]{1,0:T(8,128)S(1)}, f32[160,128]{1,0:T(8,128)S(1)}, /*index=5*/f32[128,128]{1,0:T(8,128)S(1)}, f32[96,128]{1,0:T(8,128)S(1)}) %tuple.11, ...), branch_computations={%region_0.0_spmd, %region_1.0_spmd} | conditional | bytes 8 | solution.py:373
  38.8 39.0 %careful.1 = (f32[256,192]{1,0:T(8,128)}, f32[64,128]{1,0:T(8,128)}) custom-call(f32[5,64]{1,0:T(8,128)S(1)} %get-tuple-element.26.extra_ref, f32[256,448]{1,0:T(8,128)S(1)} %get-tuple-element.27.solved_ref, f32[224,128]{1,0:T(8,128)S(1)} %get-tuple-element.28.refs_0_, f32[192,128]{1,0:T(8,128)S(1)} %get-tuple-element.29.refs_1_, ...), custom_call_target="tpu_custom_call" | custom-call | tf_op jit(solution)/shard_map/cond/branch_0_fun/careful/pallas_call | solution.py:310
  77.8 1.2 %last.2 = f32[256,128]{1,0:T(8,128)S(1)} custom-call(f32[256,192]{1,0:T(8,128)} %get-tuple-element.33.rest_ref, f32[64,128]{1,0:T(8,128)} %get-tuple-element.34.coef_ref), custom_call_target="tpu_custom_call" | custom-call | tf_op jit(solution)/shard_map/cond/branch_0_fun/last/pallas_call | solution.py:335
  79.0 0.0 copy-start
  79.0 0.6 copy-done
Async XLA Ops:
  79.0 0.7 copy-start

commit v7 on v6

--- a/solution.py
+++ b/solution.py
@@ -81,8 +81,11 @@
     size = matrix.shape[0]
     eye = identity(size)
     alpha = 2.0 / (low + high)
-    pair_ref[:size, :] = eye - alpha * matrix
-    pair_ref[size:, :] = alpha * eye
+    rho = (high - low) / (high + low)
+    scale = 2.0 / (2.0 - rho * rho)
+    residual = eye - alpha * matrix
+    pair_ref[:size, :] = (1.0 - scale) * eye + scale * mm3(residual, residual)
+    pair_ref[size:, :] = (scale * alpha) * (eye + residual)
 
     def cond(rho):
         return rho > LEAF_TOL
@@ -96,7 +99,7 @@
         pair_ref[size:, :] = scale * (pair[size:] + product[size:])
         return square / (2.0 - square)
 
-    lax.while_loop(cond, body, (high - low) / (high + low))
+    lax.while_loop(cond, body, rho * rho / (2.0 - rho * rho))
 
     @pl.when(high > 100.0 * low)
     def _():
@@ -235,11 +238,14 @@
         )
     pl.semaphore_wait(barrier, levels)
 
-    for j in range(levels):
+    for j in range(min(levels, 2)):
         copy_of(0, j).start()
     bad = jnp.zeros((1, rank), jnp.float32)
     for k in range(levels):
         copy_of(k, k).wait_recv()
+        if k == 0:
+            for j in range(2, levels):
+                copy_of(0, j).start()
         height = heights[k]
         front = own[k, k][:height, :] + landed[k, k][:height, :]
         front = unpack(front, rank, widths[k])
@@ -368,11 +374,10 @@
     rest, coef, flag = call_tree(extra, solved, blocks, inner_bits, 0)
 
     def careful():
-        return last_update(*call_tree(extra, solved, blocks, inner_bits, doublings))
-
-    return lax.cond(
-        flag[0] <= RESIDUAL_MAX, lambda: last_update(rest, coef), careful
-    )
+        return tuple(call_tree(extra, solved, blocks, inner_bits, doublings))
+
+    rest, coef = lax.cond(flag[0] <= RESIDUAL_MAX, lambda: (rest, coef), careful)
+    return last_update(rest, coef)
 
 
 def solution(mesh):

time: 79.9 us -> 77 us (0.964)
  Pallas kernels: 78.1 us -> 76 us
    pallas_call x2, Pallas kernels: 71.5 us -> 69.8 us  [call_tree(): pl.pallas_call(functools.partial(tree_kernel, rank, levels, inner_bits, d...]
where the time goes in v7:
time: 77 us; the launch traced here: 76.9 us
  Pallas kernels  76 us (99%)
    pallas_call x2, Pallas kernels, call_tree(): pl.pallas_call(functools.partial(tree_kernel, rank, levels, inner_bits, d...  69.8 us
    pallas_call x1, Pallas kernels, per_device(): pl.pallas_call(functools.partial(leaf_kernel, rank, levels), out_shape=[j...  5.33 us

profile of v7, /device:TPU:0, one launch (start us, length us, event | category | flops | bytes accessed | tf_op | source)
XLA Modules:
  0.0 76.9 jit_solution(2108944841805247994)
XLA Ops:
  0.0 5.3 %leaf.1 = (f32[256,448]{1,0:T(8,128)S(1)}, f32[5,64]{1,0:T(8,128)S(1)}, f32[224,128]{1,0:T(8,128)S(1)}, f32[192,128]{1,0:T(8,128)S(1)}, f32[160,128]{1,0:T(8,128...) custom-call(f32[256,256]{1,0:T(8,128)} %leaf_ref.1, f32[320,256]{1,0:T(8,128)} %bitcast.2, f32[256,128]{1,0:T(8,128)} %targets_ref.1, ...), custom_call_target="tpu_custom_call" | custom-call | tf_op jit(solution)/shard_map/leaf/pallas_call | solution.py:359
  5.3 31.6 %tree.1 = (f32[256,192]{1,0:T(8,128)S(1)}, f32[64,128]{1,0:T(8,128)S(1)}, f32[1]{0:T(128)}) custom-call(f32[5,64]{1,0:T(8,128)S(1)} %get-tuple-element.42.extra_ref, f32[256,448]{1,0:T(8,128)S(1)} %get-tuple-element.43.solved_ref, f32[224,128]{1,0:T(8,128)S(1)} %get-tuple-element.44.refs_0_, f32[192,128]{1,0:T(8,128)S(1)} %get-tuple-element.45.refs_1_, ...), custom_call_target="tpu_custom_call" | custom-call | tf_op jit(solution)/shard_map/tree/pallas_call | solution.py:316
  37.5 38.4 %conditional.1 = ((f32[256,192]{1,0:T(8,128)S(1)}, f32[64,128]{1,0:T(8,128)S(1)})) conditional(s32[]{:T(128)} %bitcast.1, (f32[5,64]{1,0:T(8,128)S(1)}, f32[256,448]{1,0:T(8,128)S(1)}, f32[224,128]{1,0:T(8,128)S(1)}, f32[192,128]{1,0:T(8,128)S(1)}, f32[160,128]{1,0:T(8,128)S(1)}, /*index=5*/f32[128,128]{1,0:T(8,128)S(1)}, ...), branch_computations={%region_0.0_spmd, %region_1.0_spmd} | conditional | bytes 8 | solution.py:379
  37.7 38.2 %careful.1 = (f32[256,192]{1,0:T(8,128)S(1)}, f32[64,128]{1,0:T(8,128)S(1)}) custom-call(f32[5,64]{1,0:T(8,128)S(1)} %get-tuple-element.23.extra_ref, f32[256,448]{1,0:T(8,128)S(1)} %get-tuple-element.24.solved_ref, f32[224,128]{1,0:T(8,128)S(1)} %get-tuple-element.25.refs_0_, f32[192,128]{1,0:T(8,128)S(1)} %get-tuple-element.26.refs_1_, ...), custom_call_target="tpu_custom_call" | custom-call | tf_op jit(solution)/shard_map/cond/branch_0_fun/careful/pallas_call | solution.py:316
  76.0 0.9 %last.1 = f32[256,128]{1,0:T(8,128)} custom-call(f32[256,192]{1,0:T(8,128)S(1)} %get-tuple-element.52.rest_ref, f32[64,128]{1,0:T(8,128)S(1)} %get-tuple-element.53.coef_ref), custom_call_target="tpu_custom_call" | custom-call | tf_op jit(solution)/shard_map/last/pallas_call | solution.py:341

commit v8 on v7

--- a/solution.py
+++ b/solution.py
@@ -277,13 +277,13 @@
                     bad, (FLAG_ROWS, rank)
                 )
             copy_of(k + 1, j).start()
-            if j == k + 1:
-                if k == 0:
-                    load.wait()
-                target = rest_ref if k + 2 == levels else state_ref
-                target[:, :wide] = state_ref[:, :wide] - mm(
-                    state_ref[:, wide : wide + rank], coef
-                )
+        if k + 1 < levels:
+            if k == 0:
+                load.wait()
+            target = rest_ref if k + 2 == levels else state_ref
+            target[:, :wide] = state_ref[:, :wide] - mm(
+                state_ref[:, wide : wide + rank], coef
+            )
     if not doublings:
         flag_ref[0] = jnp.max(bad)
     for pair in pairs:

time: 77 us -> 77.8 us (1.010)
  Pallas kernels: 76 us -> 76.8 us
where the time goes in v8:
time: 77.8 us; the launch traced here: 77.6 us
  Pallas kernels  76.8 us (99%)
    pallas_call x2, Pallas kernels, call_tree(): pl.pallas_call(functools.partial(tree_kernel, rank, levels, inner_bits, d...  70.6 us
    pallas_call x1, Pallas kernels, per_device(): pl.pallas_call(functools.partial(leaf_kernel, rank, levels), out_shape=[j...  5.33 us

profile of v8, /device:TPU:0, one launch (start us, length us, event | category | flops | bytes accessed | tf_op | source)
XLA Modules:
  0.0 77.6 jit_solution(5551587084754860268)
XLA Ops:
  0.0 5.3 %leaf.1 = (f32[256,448]{1,0:T(8,128)S(1)}, f32[5,64]{1,0:T(8,128)S(1)}, f32[224,128]{1,0:T(8,128)S(1)}, f32[192,128]{1,0:T(8,128)S(1)}, f32[160,128]{1,0:T(8,128...) custom-call(f32[256,256]{1,0:T(8,128)} %leaf_ref.1, f32[320,256]{1,0:T(8,128)} %bitcast.2, f32[256,128]{1,0:T(8,128)} %targets_ref.1, ...), custom_call_target="tpu_custom_call" | custom-call | tf_op jit(solution)/shard_map/leaf/pallas_call | solution.py:359
  5.3 32.0 %tree.1 = (f32[256,192]{1,0:T(8,128)S(1)}, f32[64,128]{1,0:T(8,128)S(1)}, f32[1]{0:T(128)}) custom-call(f32[5,64]{1,0:T(8,128)S(1)} %get-tuple-element.42.extra_ref, f32[256,448]{1,0:T(8,128)S(1)} %get-tuple-element.43.solved_ref, f32[224,128]{1,0:T(8,128)S(1)} %get-tuple-element.44.refs_0_, f32[192,128]{1,0:T(8,128)S(1)} %get-tuple-element.45.refs_1_, ...), custom_call_target="tpu_custom_call" | custom-call | tf_op jit(solution)/shard_map/tree/pallas_call | solution.py:316
  38.0 38.7 %conditional.1 = ((f32[256,192]{1,0:T(8,128)S(1)}, f32[64,128]{1,0:T(8,128)S(1)})) conditional(s32[]{:T(128)} %bitcast.1, (f32[5,64]{1,0:T(8,128)S(1)}, f32[256,448]{1,0:T(8,128)S(1)}, f32[224,128]{1,0:T(8,128)S(1)}, f32[192,128]{1,0:T(8,128)S(1)}, f32[160,128]{1,0:T(8,128)S(1)}, /*index=5*/f32[128,128]{1,0:T(8,128)S(1)}, ...), branch_computations={%region_0.0_spmd, %region_1.0_spmd} | conditional | bytes 8 | solution.py:379
  38.2 38.5 %careful.1 = (f32[256,192]{1,0:T(8,128)S(1)}, f32[64,128]{1,0:T(8,128)S(1)}) custom-call(f32[5,64]{1,0:T(8,128)S(1)} %get-tuple-element.23.extra_ref, f32[256,448]{1,0:T(8,128)S(1)} %get-tuple-element.24.solved_ref, f32[224,128]{1,0:T(8,128)S(1)} %get-tuple-element.25.refs_0_, f32[192,128]{1,0:T(8,128)S(1)} %get-tuple-element.26.refs_1_, ...), custom_call_target="tpu_custom_call" | custom-call | tf_op jit(solution)/shard_map/cond/branch_0_fun/careful/pallas_call | solution.py:316
  76.7 0.9 %last.1 = f32[256,128]{1,0:T(8,128)} custom-call(f32[256,192]{1,0:T(8,128)S(1)} %get-tuple-element.52.rest_ref, f32[64,128]{1,0:T(8,128)S(1)} %get-tuple-element.53.coef_ref), custom_call_target="tpu_custom_call" | custom-call | tf_op jit(solution)/shard_map/last/pallas_call | solution.py:341
